TPU v7x, 32 devices: a whole 2x2x4 slice. The times are simulated.
32 devices in a mesh: dp: 2 (over x), ctx: 4 (over y, core), tensor: 4 (over z).
Axes of the slice: x: 2, y: 2, z: 4, core: 2. Of those that a mesh axis runs over, the one named last changes fastest.
Arguments:
- tokens: bfloat16 [8192, 768], P(('dp', 'ctx', 'tensor')), may hold values from -6 to 6
- lengths: int32 [2, 5], P('dp'), may hold values from 0 to 3892, as said below
- gain_attn: bfloat16 [768], P('dp'), may hold values from 0.099609375 to 1.8984375
- w_qkv: bfloat16 [3, 768, 768], P(None, 'dp', 'tensor'), may hold values from -0.21875 to 0.21875
- w_out: bfloat16 [768, 768], P('tensor', 'dp'), may hold values from -1.75 to 1.75
- gain_mlp: bfloat16 [768], P('dp'), may hold values from 0.099609375 to 1.8984375
- w_in: bfloat16 [2, 768, 1152], P(None, 'dp', 'tensor'), may hold values from -0.21875 to 0.21875
- w_down: bfloat16 [1152, 768], P('tensor', 'dp'), may hold values from -0.1875 to 0.1875
- cotangent: bfloat16 [8192, 768], P(('dp', 'ctx', 'tensor')), may hold values from -6 to 6
Outputs:
- activations: bfloat16 [8192, 768], P(('dp', 'ctx', 'tensor'))
- grad_tokens: bfloat16 [8192, 768], P(('dp', 'ctx', 'tensor'))
- grad_gain_attn: float32 [768], P('dp')
- grad_w_qkv: float32 [3, 768, 768], P(None, 'dp', 'tensor')
- grad_w_out: float32 [768, 768], P('tensor', 'dp')
- grad_gain_mlp: float32 [768], P('dp')
- grad_w_in: float32 [2, 768, 1152], P(None, 'dp', 'tensor')
- grad_w_down: float32 [1152, 768], P('tensor', 'dp')
Inputs may be any that keep to these rules, and one draw needn't show every extreme that they name: Row s lists in order the lengths of the documents packed into sequence s, followed by zeros where it has fewer than 5; each row sums to 4096; each row holds one document longer than 3072, and its other documents have 1024 // 5 to 255 tokens (at least 1).
All inputs are finite; a program needn't handle non-finite values.
Results may differ from a plain program's by a relative error of at most 0.025.
Values may be sent and summed in bfloat16 or wider, within the bound.
No kernel may reach another device: no remote copies, remote signals or barrier semaphores. Data moves between devices by JAX's collectives and lax.ppermute only.
A program may use at most 128 MiB of HBM per device.

v0:
```python
import math

import jax
import jax.numpy as jnp
from jax import lax
from jax.sharding import PartitionSpec as P

HEAD_DIM = 64


EPSILON = 1e-05
ROPE_BASE = 160000.0
MASKED = -1e30


def segment_of(positions, doc_lengths):
    bounds = jnp.cumsum(doc_lengths)
    return jnp.sum((positions[:, None] >= bounds[None, :]).astype(jnp.int32), axis=1)


def rope_tables(positions):
    halves = HEAD_DIM // 2
    exponent = jnp.arange(halves, dtype=jnp.float32) * (2.0 / HEAD_DIM)
    inverse = ROPE_BASE ** (-exponent)
    angles = positions.astype(jnp.float32)[:, None] * inverse[None, :]
    return (jnp.cos(angles), jnp.sin(angles))


def rotate(values, cosine, sine_table):
    halves = values.shape[-1] // 2
    first = values[..., :halves]
    second = values[..., halves:]
    cos_wide = cosine[:, None, :]
    sin_wide = sine_table[:, None, :]
    return jnp.concatenate(
        [first * cos_wide - second * sin_wide, second * cos_wide + first * sin_wide], axis=-1
    )


def unrotate(values, cosine, sine_table):
    halves = values.shape[-1] // 2
    first = values[..., :halves]
    second = values[..., halves:]
    cos_wide = cosine[:, None, :]
    sin_wide = sine_table[:, None, :]
    return jnp.concatenate(
        [first * cos_wide + second * sin_wide, second * cos_wide - first * sin_wide], axis=-1
    )


def norm_parts(values, gain):
    centre = values - jnp.mean(values, axis=-1, keepdims=True)
    spread = jnp.mean(centre * centre, axis=-1, keepdims=True)
    scaling = lax.rsqrt(spread + EPSILON)
    normal = centre * scaling
    return (normal * gain, normal, scaling)


def norm_back(incoming, normal, scaling, gain):
    scaled = incoming * gain
    grad_gain = jnp.sum(incoming * normal, axis=0)
    grad_values = scaling * (
        scaled
        - jnp.mean(scaled, axis=-1, keepdims=True)
        - normal * jnp.mean(scaled * normal, axis=-1, keepdims=True)
    )
    return (grad_gain, grad_values)


def gelu_exact(values):
    return jax.nn.gelu(values, approximate=False)


def local(tokens, lengths, gain_attn, w_qkv, w_out, gain_mlp, w_in, w_down, cotangent):
    share_rows = tokens.shape[0]
    rows_bf, upstream = (
        lax.all_gather(tokens, "tensor", axis=0, tiled=True),
        lax.all_gather(cotangent, "tensor", axis=0, tiled=True),
    )
    local_rows = rows_bf.shape[0]
    gain_one, qkv_full, out_full, gain_two, full_input_weight, down_full = (
        lax.all_gather(gain_attn, "dp", axis=0, tiled=True),
        lax.all_gather(w_qkv, "dp", axis=1, tiled=True),
        lax.all_gather(w_out, "dp", axis=1, tiled=True),
        lax.all_gather(gain_mlp, "dp", axis=0, tiled=True),
        lax.all_gather(w_in, "dp", axis=1, tiled=True),
        lax.all_gather(w_down, "dp", axis=1, tiled=True),
    )
    inputs = rows_bf.astype(jnp.float32)
    gain_one32 = gain_one.astype(jnp.float32)
    gain_two32 = gain_two.astype(jnp.float32)
    normed, normal_one, scaling_one = norm_parts(inputs, gain_one32)
    normed_bf = normed.astype(jnp.bfloat16)
    project = jnp.einsum("rd,tdc->trc", normed_bf, qkv_full, preferred_element_type=jnp.float32)
    local_width = qkv_full.shape[2]
    local_heads = local_width // HEAD_DIM
    head_shape = (local_rows, local_heads, HEAD_DIM)
    positions = lax.axis_index("ctx") * local_rows + jnp.arange(local_rows, dtype=jnp.int32)
    cosine, sine_table = rope_tables(positions)
    queries = rotate(project[0].reshape(head_shape), cosine, sine_table).astype(jnp.bfloat16)
    keys_rot = (
        rotate(project[1].reshape(head_shape), cosine, sine_table)
        .astype(jnp.bfloat16)
        .reshape(local_rows, local_width)
    )
    values_bf = project[2].astype(jnp.bfloat16)
    doc_lengths = lengths[0]
    query_segments = segment_of(positions, doc_lengths)
    score_scale = HEAD_DIM ** (-0.5)

    def block_scores(key_block, key_first):
        key_count = key_block.shape[0]
        key_positions = key_first + jnp.arange(key_count, dtype=jnp.int32)
        same_doc = query_segments[:, None] == segment_of(key_positions, doc_lengths)[None, :]
        scores = (
            jnp.einsum("qhd,khd->hqk", queries, key_block, preferred_element_type=jnp.float32)
            * score_scale
        )
        return jnp.where(same_doc[None], scores, MASKED)

    def split_blocks(key_piece, value_piece, first_row):
        piece_rows = key_piece.shape[0]
        block_row_span = math.gcd(piece_rows, 512)
        block_count = piece_rows // block_row_span
        key_blocks = key_piece.reshape(block_count, block_row_span, local_heads, HEAD_DIM)
        value_blocks = value_piece.reshape(block_count, block_row_span, local_heads, HEAD_DIM)
        block_firsts = first_row + jnp.arange(block_count, dtype=jnp.int32) * block_row_span
        return (key_blocks, value_blocks, block_firsts)

    initial = (
        jnp.full((local_heads, local_rows), MASKED, jnp.float32),
        jnp.zeros((local_heads, local_rows), jnp.float32),
        jnp.zeros((local_heads, local_rows, HEAD_DIM), jnp.float32),
    )
    key_blocks, value_blocks, block_firsts = split_blocks(
        lax.all_gather(keys_rot, "ctx", axis=0, tiled=True),
        lax.all_gather(values_bf, "ctx", axis=0, tiled=True),
        jnp.int32(0),
    )

    def accumulate(running_state, item_blocks):
        maxima, totals, weighted = running_state
        key_block, value_block, key_first = item_blocks
        scores = block_scores(key_block, key_first)
        new_max = jnp.maximum(maxima, jnp.max(scores, axis=-1))
        factor = jnp.exp(maxima - new_max)
        exponent_vals = jnp.exp(scores - new_max[..., None])
        totals = totals * factor + jnp.sum(exponent_vals, axis=-1)
        weighted = weighted * factor[..., None] + jnp.einsum(
            "hqk,khd->hqd",
            exponent_vals.astype(jnp.bfloat16),
            value_block,
            preferred_element_type=jnp.float32,
        )
        return ((new_max, totals, weighted), None)

    maxima, totals, weighted = lax.scan(
        accumulate, initial, (key_blocks, value_blocks, block_firsts)
    )[0]
    heads_f32 = weighted / totals[..., None]
    logsum = maxima + jnp.log(totals)
    heads_bf = (
        jnp.transpose(heads_f32, (1, 0, 2)).reshape(local_rows, local_width).astype(jnp.bfloat16)
    )
    attn_part = jnp.dot(heads_bf, out_full, preferred_element_type=jnp.float32)
    attn_share = lax.psum_scatter(
        attn_part.astype(jnp.bfloat16), "tensor", scatter_dimension=0, tiled=True
    ).astype(jnp.float32)
    hidden_share = tokens.astype(jnp.float32) + attn_share
    hidden = lax.all_gather(hidden_share.astype(jnp.bfloat16), "tensor", axis=0, tiled=True).astype(
        hidden_share.dtype
    )
    normed_two, normal_two, scaling_two = norm_parts(hidden, gain_two32)
    second_normed_half_precision = normed_two.astype(jnp.bfloat16)
    inner_out = jnp.einsum(
        "gi,eiv->egv",
        second_normed_half_precision,
        full_input_weight,
        preferred_element_type=jnp.float32,
    )
    activated, gelu_back = jax.vjp(gelu_exact, inner_out[0])
    product_bf = (activated * inner_out[1]).astype(jnp.bfloat16)
    branch_part = jnp.dot(product_bf, down_full, preferred_element_type=jnp.float32)
    branch_share = lax.psum_scatter(
        branch_part.astype(jnp.bfloat16), "tensor", scatter_dimension=0, tiled=True
    ).astype(jnp.float32)
    activations = (hidden_share + branch_share).astype(jnp.bfloat16)
    grad_down = jnp.einsum("rf,rd->fd", product_bf, upstream, preferred_element_type=jnp.float32)
    grad_product = jnp.einsum("rd,fd->rf", upstream, down_full, preferred_element_type=jnp.float32)
    grad_first = gelu_back(grad_product * inner_out[1])[0]
    inner_gradient = jnp.stack([grad_first, grad_product * activated]).astype(jnp.bfloat16)
    grad_in = jnp.einsum(
        "pb,opv->obv",
        second_normed_half_precision,
        inner_gradient,
        preferred_element_type=jnp.float32,
    )
    normed_two_part = jnp.einsum(
        "bxq,byq->xy", inner_gradient, full_input_weight, preferred_element_type=jnp.float32
    )
    grad_normed_two = lax.psum(normed_two_part.astype(jnp.bfloat16), "tensor").astype(jnp.float32)
    grad_gain_two, grad_hidden_norm = norm_back(
        grad_normed_two, normal_two, scaling_two, gain_two32
    )
    grad_hidden = upstream.astype(jnp.float32) + grad_hidden_norm
    hidden_grad_bf = grad_hidden.astype(jnp.bfloat16)
    grad_out = jnp.einsum("rc,rd->cd", heads_bf, hidden_grad_bf, preferred_element_type=jnp.float32)
    grad_heads = (
        jnp.einsum("rd,cd->rc", hidden_grad_bf, out_full, preferred_element_type=jnp.float32)
        .astype(jnp.bfloat16)
        .reshape(head_shape)
    )
    row_delta = jnp.sum(
        jnp.transpose(grad_heads.astype(jnp.float32), (1, 0, 2)) * heads_f32, axis=-1
    )
    whole_keys, whole_values = (
        lax.all_gather(keys_rot, "ctx", axis=0, tiled=True),
        lax.all_gather(values_bf, "ctx", axis=0, tiled=True),
    )
    seq_rows = whole_keys.shape[0]
    key_blocks, value_blocks, block_firsts = split_blocks(whole_keys, whole_values, 0)
    block_row_span = key_blocks.shape[1]

    def backstep(grad_queries, item_blocks):
        key_block, value_block, key_first = item_blocks
        scores = block_scores(key_block, key_first)
        probs_exact = jnp.exp(scores - logsum[..., None])
        grad_probs = jnp.einsum(
            "qhd,khd->hqk", grad_heads, value_block, preferred_element_type=jnp.float32
        )
        grad_scores = (probs_exact * (grad_probs - row_delta[..., None])).astype(jnp.bfloat16)
        grad_queries = (
            grad_queries
            + jnp.einsum("hqk,khd->qhd", grad_scores, key_block, preferred_element_type=jnp.float32)
            * score_scale
        )
        grad_keys = (
            jnp.einsum("hqk,qhd->khd", grad_scores, queries, preferred_element_type=jnp.float32)
            * score_scale
        )
        grad_values = jnp.einsum(
            "hqk,qhd->khd",
            probs_exact.astype(jnp.bfloat16),
            grad_heads,
            preferred_element_type=jnp.float32,
        )
        joined = jnp.concatenate(
            [
                grad_keys.reshape(block_row_span, local_width),
                grad_values.reshape(block_row_span, local_width),
            ],
            axis=1,
        )
        return (grad_queries, joined)

    grad_queries, key_terms = lax.scan(
        backstep, jnp.zeros(head_shape, jnp.float32), (key_blocks, value_blocks, block_firsts)
    )
    key_terms = key_terms.reshape(seq_rows, 2 * local_width)
    key_grads = lax.psum_scatter(
        key_terms.astype(jnp.bfloat16), "ctx", scatter_dimension=0, tiled=True
    ).astype(jnp.float32)
    grad_keys_own = unrotate(key_grads[:, :local_width].reshape(head_shape), cosine, sine_table)
    owned_query_gradient = unrotate(grad_queries, cosine, sine_table)
    grad_project = jnp.stack(
        [
            owned_query_gradient.reshape(local_rows, local_width),
            grad_keys_own.reshape(local_rows, local_width),
            key_grads[:, local_width:],
        ]
    ).astype(jnp.bfloat16)
    grad_qkv = jnp.einsum(
        "rd,trc->tdc", normed_bf, grad_project, preferred_element_type=jnp.float32
    )
    normed_part = jnp.einsum(
        "trc,tdc->rd", grad_project, qkv_full, preferred_element_type=jnp.float32
    )
    grad_normed = lax.psum(normed_part.astype(jnp.bfloat16), "tensor").astype(jnp.float32)
    grad_gain_one, grad_input_norm = norm_back(grad_normed, normal_one, scaling_one, gain_one32)
    grad_inputs = grad_hidden + grad_input_norm
    grad_tokens = lax.dynamic_slice_in_dim(
        grad_inputs, lax.axis_index("tensor") * share_rows, share_rows, 0
    ).astype(jnp.bfloat16)
    gradients = (grad_gain_one, grad_qkv, grad_out, grad_gain_two, grad_in, grad_down)
    gradients = (
        lax.psum(gradients[0].astype(jnp.bfloat16), "ctx").astype(jnp.float32),
        lax.psum(gradients[1].astype(jnp.bfloat16), "ctx").astype(jnp.float32),
        lax.psum(gradients[2].astype(jnp.bfloat16), "ctx").astype(jnp.float32),
        lax.psum(gradients[3].astype(jnp.bfloat16), "ctx").astype(jnp.float32),
        lax.psum(gradients[4].astype(jnp.bfloat16), "ctx").astype(jnp.float32),
        lax.psum(gradients[5].astype(jnp.bfloat16), "ctx").astype(jnp.float32),
    )
    gradients = (
        lax.psum_scatter(
            gradients[0].astype(jnp.bfloat16), "dp", scatter_dimension=0, tiled=True
        ).astype(jnp.float32),
        lax.psum_scatter(
            gradients[1].astype(jnp.bfloat16), "dp", scatter_dimension=1, tiled=True
        ).astype(jnp.float32),
        lax.psum_scatter(
            gradients[2].astype(jnp.bfloat16), "dp", scatter_dimension=1, tiled=True
        ).astype(jnp.float32),
        lax.psum_scatter(
            gradients[3].astype(jnp.bfloat16), "dp", scatter_dimension=0, tiled=True
        ).astype(jnp.float32),
        lax.psum_scatter(
            gradients[4].astype(jnp.bfloat16), "dp", scatter_dimension=1, tiled=True
        ).astype(jnp.float32),
        lax.psum_scatter(
            gradients[5].astype(jnp.bfloat16), "dp", scatter_dimension=1, tiled=True
        ).astype(jnp.float32),
    )
    return (
        activations,
        grad_tokens,
        gradients[0],
        gradients[1],
        gradients[2],
        gradients[3],
        gradients[4],
        gradients[5],
    )


def solution(mesh):
    return jax.shard_map(
        local,
        mesh=mesh,
        in_specs=(
            P(("dp", "ctx", "tensor"), None),
            P("dp", None),
            P("dp"),
            P(None, "dp", "tensor"),
            P("tensor", "dp"),
            P("dp"),
            P(None, "dp", "tensor"),
            P("tensor", "dp"),
            P(("dp", "ctx", "tensor"), None),
        ),
        out_specs=(
            P(("dp", "ctx", "tensor"), None),
            P(("dp", "ctx", "tensor"), None),
            P("dp"),
            P(None, "dp", "tensor"),
            P("tensor", "dp"),
            P("dp"),
            P(None, "dp", "tensor"),
            P("tensor", "dp"),
        ),
        check_vma=False,
    )
```

profile of v0, /device:TPU:0, one launch (start us, length us, event | category | flops | bytes accessed | tf_op | source)
XLA Modules:
  0.0 743.4 jit_solution(7835819673659409643)
XLA Ops:
  8.6 5.2 all-gather.1
  13.9 12.0 %all_gather.37 = bf16[3,768,192]{1,2,0:T(8,128)(2,1)S(1)} all-gather(bf16[3,384,192]{1,2,0:T(8,128)(2,1)} %param.16), channel_id=1, replica_groups=mesh['dp'=2,'ctx'=4,'tensor'=4] {'dp'}, dimensions={1}, use_global_device_ids=true | all-gather | bytes 1327104 | tf_op jit(solution)/shard_map/all_gather | solution.py:83
  25.9 23.5 %all-gather.9.cloned.1.call-done = bf16[1024,768]{1,0:T(8,128)(2,1)} async-done(((bf16[256,768]{1,0:T(8,128)(2,1)}), bf16[1024,768]{1,0:T(8,128)(2,1)}) %all-gather.9.cloned.1.call-update) | async-done | bytes 1572880 | tf_op jit(solution)/shard_map/all_gather | solution.py:77
  56.9 6.2 all_gather.40
  63.3 9.5 %all-gather.17.cloned.1.call-done = bf16[1,4096,192]{1,2,0:T(8,128)(2,1)} async-done(((bf16[1,1024,192]{1,2,0:T(8,128)(2,1)}), bf16[1,4096,192]{1,2,0:T(8,128)(2,1)}) %all-gather.17.cloned.1.call-update) | async-done | bytes 1572880 | tf_op jit(solution)/shard_map/all_gather | solution.py:137
  76.5 18.1 %all-gather.11.cloned.1.call-done = bf16[4096,192]{0,1:T(8,128)(2,1)} async-done(((bf16[1024,192]{0,1:T(8,128)(2,1)}), bf16[4096,192]{0,1:T(8,128)(2,1)}) %all-gather.11.cloned.1.call-update) | async-done | bytes 1572880 | tf_op jit(solution)/shard_map/all_gather | solution.py:136
  97.2 59.8 %while.32 = (s32[]{:T(128)}, f32[3,1024]{1,0:T(4,128)S(1)}, f32[3,1024]{1,0:T(4,128)S(1)}, f32[3,1024,64]{1,2,0:T(8,128)S(1)}, s32[1024]{0:T(1024)S(1)}, /*index...) while((s32[]{:T(128)}, f32[3,1024]{1,0:T(4,128)S(1)}, ...), condition=%wide.region_9.10_spmd.clone, body=%wide.region_5.0_spmd.clone.sunk | while | flops 421091840 | bytes 23539892 | solution.py:157
  101.7 2.9 fusion.163
  109.2 2.9 fusion.163
  116.7 2.9 fusion.163
  124.1 2.9 fusion.163
  139.1 2.9 fusion.163
  146.6 2.9 fusion.163
  154.1 2.9 fusion.163
  162.7 34.8 %reduce-scatter.16.cloned.1.call-done = bf16[256,768]{1,0:T(8,128)(2,1)} async-done(((bf16[1024,768]{1,0:T(8,128)(2,1)}), bf16[256,768]{1,0:T(8,128)(2,1)}) %reduce-scatter.16.cloned.1.call-update) | async-done | bytes 393232 | tf_op jit(solution)/shard_map/reduce_scatter | solution.py:166
  199.4 4.3 all-gather.2
  203.8 6.6 all_gather.44
  210.4 10.2 %all_gather.43 = bf16[2,768,288]{1,2,0:T(8,128)(2,1)} all-gather(bf16[2,384,288]{1,2,0:T(8,128)(2,1)S(1)} %copy-done.31), channel_id=1, replica_groups=mesh['dp'=2,'ctx'=4,'tensor'=4] {'dp'}, dimensions={1}, use_global_device_ids=true | all-gather | bytes 1327104 | tf_op jit(solution)/shard_map/all_gather | solution.py:86
  220.6 14.4 %all-gather.15.cloned.1.call-done = bf16[1024,768]{1,0:T(8,128)(2,1)} async-done(((bf16[256,768]{1,0:T(8,128)(2,1)}), bf16[1024,768]{1,0:T(8,128)(2,1)}) %all-gather.15.cloned.1.call-update) | async-done | bytes 1572880 | tf_op jit(solution)/shard_map/all_gather | solution.py:78
  235.0 3.1 fusion.113
  238.1 34.9 %all-gather.13.cloned.1.call-done = bf16[1024,768]{1,0:T(8,128)(2,1)} async-done(((bf16[256,768]{1,0:T(8,128)(2,1)}), bf16[1024,768]{1,0:T(8,128)(2,1)}) %all-gather.13.cloned.1.call-update) | async-done | bytes 1572880 | tf_op jit(solution)/shard_map/all_gather | solution.py:170
  285.1 66.7 %all-reduce.9.cloned.1.call-done = bf16[1024,768]{1,0:T(8,128)(2,1)} async-done(((bf16[1024,768]{1,0:T(8,128)(2,1)}), bf16[1024,768]{1,0:T(8,128)(2,1)}) %all-reduce.9.cloned.1.call-update) | async-done | bytes 1572880 | tf_op jit(solution)/shard_map/psum | solution.py:201
  351.8 3.7 fusion.57
  359.6 103.7 %while.33 = (s32[]{:T(128)}, f32[1024,3,64]{0,2,1:T(8,128)S(1)}, bf16[8,512,384]{1,2,0:T(8,128)(2,1)}, bf16[8,512,3,64]{1,3,2,0:T(8,128)(2,1)}, s32[1024]{0:T(10...) while((s32[]{:T(128)}, f32[1024,3,64]{0,2,1:T(8,128)S(1)}, ...), condition=%wide.region_20.21_spmd.clone, body=%wide.region_18.20_spmd.clone.sunk | while | flops 1024466432 | bytes 36520220 | solution.py:256
  365.8 3.2 fusion.175
  378.7 3.2 fusion.175
  391.7 3.2 fusion.175
  404.6 3.2 fusion.175
  417.6 3.2 fusion.175
  430.6 3.2 fusion.175
  443.6 3.2 fusion.175
  456.6 3.2 fusion.175
  463.3 4.0 copy.63
  467.4 3.0 convolution_convert_fusion.3
  472.5 8.8 %reduce-scatter.26.cloned.1.call-start = ((), (), s32[]{:S(2)}) async-start(), calls=%async_computation.19 | async-start | bytes 1474560
  481.4 3.5 fusion.65
  484.8 3.5 copy.59
  495.8 8.7 %reduce-scatter.20.cloned.1.call-done = bf16[1024,384]{0,1:T(8,128)(2,1)} async-done(((bf16[4096,384]{0,1:T(8,128)(2,1)}), bf16[1024,384]{0,1:T(8,128)(2,1)}) %reduce-scatter.20.cloned.1.call-update) | async-done | bytes 786448 | tf_op jit(solution)/shard_map/reduce_scatter | solution.py:260
  515.7 4.1 reshape.289
  524.0 20.0 %reduce-scatter.26.cloned.1.call-done = bf16[384,576]{1,0:T(8,128)(2,1)} async-done(((bf16[768,576]{1,0:T(8,128)(2,1)}), bf16[384,576]{1,0:T(8,128)(2,1)}) %reduce-scatter.26.cloned.1.call-update) | async-done | bytes 442384
  547.8 12.2 %reduce-scatter.24.cloned.1.call-done = bf16[384,192]{1,0:T(8,128)(2,1)} async-done(((bf16[768,192]{1,0:T(8,128)(2,1)}), bf16[384,192]{1,0:T(8,128)(2,1)}) %reduce-scatter.24.cloned.1.call-update) | async-done | bytes 147472
  561.8 35.8 %reduce-scatter.18.cloned.1.call-done = bf16[256,768]{1,0:T(8,128)(2,1)} async-done(((bf16[1024,768]{1,0:T(8,128)(2,1)}), bf16[256,768]{1,0:T(8,128)(2,1)}) %reduce-scatter.18.cloned.1.call-update) | async-done | bytes 393232 | tf_op jit(solution)/shard_map/reduce_scatter | solution.py:184
  599.4 68.6 %all-reduce.11.cloned.1.call-done = bf16[1024,768]{1,0:T(8,128)(2,1)} async-done(((bf16[1024,768]{1,0:T(8,128)(2,1)}), bf16[1024,768]{1,0:T(8,128)(2,1)}) %all-reduce.11.cloned.1.call-update) | async-done | bytes 1572880 | tf_op jit(solution)/shard_map/psum | solution.py:278
  668.0 4.7 fusion.58
  672.7 5.0 all-reduce.4
  677.8 6.0 all-reduce.2
  685.0 3.8 reduce-scatter.22.cloned.1.call-done
  694.9 36.4 %all-reduce.13.cloned.1.call-done = (bf16[3,384,192]{1,2,0:T(8,128)(2,1)}, bf16[192,384]{1,0:T(8,128)(2,1)}, bf16[2,384,288]{1,2,0:T(8,128)(2,1)}, bf16[288,384]{1,0:T(8,128)(2,1)}) async-done(((bf16[3,384,192]{1,2,0:T(8,128)(2,1)}, bf16[192,384]{1,0:T(8,128)(2,1)}, bf16[2,384,288]{1,2,0:T(8,128)(2,1)}, bf16[288,384]{1,0:T(8,128)(2,1)}), (bf16[3,384,192]{1,2,0:T(8,128)(2,1)}, bf16[192,384]{1,0:T(8,128)(2,1)}, ...) | async-done | bytes 1253392 | tf_op jit(solution)/shard_map/psum | solution.py:287
  (421 shorter events, 199.1 us)
Async XLA Ops:
  7.2 42.2 %all-gather.9.cloned.1.call-start = ((), (), s32[]{:S(2)}) async-start(), calls=%async_computation.7 | async-start | bytes 1966080 | tf_op jit(solution)/shard_map/all_gather | solution.py:77
  7.9 64.9 %all-gather.17.cloned.1.call-start = ((), (), s32[]{:S(2)}) async-start(), calls=%async_computation.16 | async-start | bytes 1966080 | tf_op jit(solution)/shard_map/all_gather | solution.py:137
  13.9 38.1 %copy-start.51 = (f32[768]{0:T(1024)}, f32[768]{0:T(1024)S(1)}, u32[]{:S(2)}) copy-start(f32[768]{0:T(1024)S(1)} %reshape.279) | copy-start | bytes 9220
  25.9 26.1 %copy-start.23 = (bf16[3,768,192]{1,2,0:T(8,128)(2,1)}, bf16[3,768,192]{1,2,0:T(8,128)(2,1)S(1)}, u32[]{:S(2)}) copy-start(bf16[3,768,192]{1,2,0:T(8,128)(2,1)S(1)} %all_gather.37) | copy-start | bytes 2654212
  54.1 40.5 %all-gather.11.cloned.1.call-start = ((), (), s32[]{:S(2)}) async-start(), calls=%async_computation.8 | async-start | bytes 1966080 | tf_op jit(solution)/shard_map/all_gather | solution.py:136
  56.5 141.0 %reduce-scatter.16.cloned.1.call-start = ((), (), s32[]{:S(2)}) async-start(), calls=%async_computation.9 | async-start | bytes 1966080 | tf_op jit(solution)/shard_map/reduce_scatter | solution.py:166
  157.0 4.9 copy-start.4
  157.0 4.9 copy-start.21
  157.0 4.9 copy-start.29
  157.1 4.9 copy-start.40
  157.1 4.9 copy-start.59
  159.1 38.4 %copy-start.8 = (bf16[256,768]{1,0:T(8,128)(2,1)S(1)}, bf16[256,768]{1,0:T(8,128)(2,1)}, u32[]{:S(2)}) copy-start(bf16[256,768]{1,0:T(8,128)(2,1)} %param.13) | copy-start | bytes 1179652
  162.0 37.4 %copy-start.56 = (bf16[384]{0:T(512)(128)(2,1)S(1)}, bf16[384]{0:T(512)(128)(2,1)}, u32[]{:S(2)}) copy-start(bf16[384]{0:T(512)(128)(2,1)} %param.18) | copy-start | bytes 2308
  162.0 41.8 %copy-start.35 = (bf16[288,384]{1,0:T(8,128)(2,1)S(1)}, bf16[288,384]{1,0:T(8,128)(2,1)}, u32[]{:S(2)}) copy-start(bf16[288,384]{1,0:T(8,128)(2,1)} %param.20) | copy-start | bytes 663556
  162.0 48.4 %copy-start.31 = (bf16[2,384,288]{1,2,0:T(8,128)(2,1)S(1)}, bf16[2,384,288]{1,2,0:T(8,128)(2,1)}, u32[]{:S(2)}) copy-start(bf16[2,384,288]{1,2,0:T(8,128)(2,1)} %param.19) | copy-start | bytes 1327108
  162.0 73.0 %all-gather.15.cloned.1.call-start = ((), (), s32[]{:S(2)}) async-start(), calls=%async_computation.12 | async-start | bytes 1966080 | tf_op jit(solution)/shard_map/all_gather | solution.py:78
  162.6 110.4 %all-gather.13.cloned.1.call-start = ((), (), s32[]{:S(2)}) async-start(), calls=%async_computation.10 | async-start | bytes 1966080 | tf_op jit(solution)/shard_map/all_gather | solution.py:170
  199.3 152.5 %all-reduce.9.cloned.1.call-start = ((), (), s32[]{:S(2)}) async-start(), calls=%async_computation.13 | async-start | bytes 3145728 | tf_op jit(solution)/shard_map/psum | solution.py:201
  203.8 71.7 %copy-start.42 = (f32[768]{0:T(1024)}, f32[768]{0:T(1024)S(1)}, u32[]{:S(2)}) copy-start(f32[768]{0:T(1024)S(1)} %reshape.280) | copy-start | bytes 9220
  210.4 27.7 %copy-start.12 = (bf16[288,768]{1,0:T(8,128)(2,1)}, bf16[288,768]{1,0:T(8,128)(2,1)S(1)}, u32[]{:S(2)}) copy-start(bf16[288,768]{1,0:T(8,128)(2,1)S(1)} %all_gather.44) | copy-start | bytes 1327108
  273.0 2.5 copy-start.25
  281.1 2.6 copy-start.27
  283.7 220.8 %reduce-scatter.20.cloned.1.call-start = ((), (), s32[]{:S(2)}) async-start(), calls=%async_computation.14 | async-start | bytes 3932160 | tf_op jit(solution)/shard_map/reduce_scatter | solution.py:260
  285.1 70.5 %copy-start.39 = (f32[1024]{0:T(1024)S(1)}, f32[1024]{0:T(1024)}, u32[]{:S(2)}) copy-start(f32[1024]{0:T(1024)} %copy-done.38) | copy-start | bytes 12292
  285.1 70.5 %copy-start.43 = (f32[768]{0:T(1024)S(1)}, f32[768]{0:T(1024)}, u32[]{:S(2)}) copy-start(f32[768]{0:T(1024)} %copy-done.42) | copy-start | bytes 9220
  285.1 70.5 %copy-start.47 = (f32[1024]{0:T(1024)S(1)}, f32[1024]{0:T(1024)}, u32[]{:S(2)}) copy-start(f32[1024]{0:T(1024)} %copy-done.46) | copy-start | bytes 12292
  351.8 3.8 copy-start.6
  351.8 3.8 copy-start.7
  467.4 54.8 %reduce-scatter.28.cloned.1.call-start = ((), (), s32[]{:S(2)}) async-start(), calls=%async_computation.20 | async-start | bytes 884736
  470.4 11.0 %copy-start.48 = (f32[1024]{0:T(1024)S(1)}, f32[1024]{0:T(1024)}, u32[]{:S(2)}) copy-start(f32[1024]{0:T(1024)} %copy-done.46) | copy-start | bytes 12292
  472.5 71.5 %reduce-scatter.26.cloned.1.call-start = ((), (), s32[]{:S(2)}) async-start(), calls=%async_computation.19 | async-start | bytes 1474560
  490.0 3.5 copy-start.13
  490.0 3.5 copy-start.26
  490.1 70.0 %reduce-scatter.24.cloned.1.call-start = ((), (), s32[]{:S(2)}) async-start(), calls=%async_computation.18 | async-start | bytes 589824
  493.5 104.0 %reduce-scatter.18.cloned.1.call-start = ((), (), s32[]{:S(2)}) async-start(), calls=%async_computation.11 | async-start | bytes 1966080 | tf_op jit(solution)/shard_map/reduce_scatter | solution.py:184
  495.8 10.0 %copy-start.18 = (f32[1024,32]{0,1:T(8,128)S(1)}, f32[1024,32]{0,1:T(8,128)}, u32[]{:S(2)}) copy-start(f32[1024,32]{0,1:T(8,128)} %copy-done.17) | copy-start | bytes 393220
  495.8 10.0 %copy-start.20 = (f32[1024,32]{0,1:T(8,128)S(1)}, f32[1024,32]{0,1:T(8,128)}, u32[]{:S(2)}) copy-start(f32[1024,32]{0,1:T(8,128)} %copy-done.19) | copy-start | bytes 393220
  495.8 172.3 %all-reduce.11.cloned.1.call-start = ((), (), s32[]{:S(2)}) async-start(), calls=%async_computation.15 | async-start | bytes 3145728 | tf_op jit(solution)/shard_map/psum | solution.py:278
  507.0 2.8 copy-start.45
  507.0 2.8 copy-start.50
  507.0 2.8 copy-start.52
  509.7 179.1 %reduce-scatter.22.cloned.1.call-start = ((), (), s32[]{:S(2)}) async-start(), calls=%async_computation.17 | async-start | bytes 1474560
  515.7 4.2 copy-start.58
  519.9 77.7 %copy-start.16 = (bf16[256,768]{1,0:T(8,128)(2,1)S(1)}, bf16[256,768]{1,0:T(8,128)(2,1)}, u32[]{:S(2)}) copy-start(bf16[256,768]{1,0:T(8,128)(2,1)} %reduce-scatter.16.cloned.1.call-done) | copy-start | bytes 1179652
  519.9 211.4 %all-reduce.13.cloned.1.call-start = ((), (), s32[]{:S(2)}) async-start(), calls=%async_computation.21 | async-start | bytes 2506752 | tf_op jit(solution)/shard_map/psum | solution.py:287
  599.4 73.3 %copy-start.55 = (bf16[768]{0:T(1024)(128)(2,1)S(1)}, bf16[768]{0:T(1024)(128)(2,1)}, u32[]{:S(2)}) copy-start(bf16[768]{0:T(1024)(128)(2,1)} %get-tuple-element.430) | copy-start | bytes 4612
  731.2 3.7 copy-start.36
  731.2 4.5 copy-start.32
  (48 other events, 81.5 us)
Sparse Core Ops, SparseCore 0:
  9.6 39.7 all-gather.8
  54.2 18.5 all-gather.16
  74.9 19.6 all-gather.10
  162.1 35.2 reduce-scatter.15
  198.9 36.0 all-gather.14
  237.0 35.9 all-gather.12
  283.8 67.9 all-reduce.8
  467.5 36.9 reduce-scatter.19
  506.9 15.2 reduce-scatter.27
  524.3 19.6 reduce-scatter.25
  546.9 13.1 reduce-scatter.23
  562.2 35.2 reduce-scatter.17
  599.9 68.0 all-reduce.10
  670.1 18.6 reduce-scatter.21
  692.2 38.9 all-reduce.12
where the time goes:
time: 754 us; the launch traced here: 743 us
  waiting for transfers between devices  389 us (52%)
  matrix products  141 us (19%)
  other arithmetic  72.8 us (10%)
  local copies, waits for them, and re-layouts  58.1 us (8%)
  blocking collectives  55.6 us (7%)
  between operations  15.6 us (2%)
  starting transfers between devices  9.65 us (1%)
    psum x1, waiting for transfers between devices, local(): lax.psum(normed_part.astype(jnp.bfloat16), 'tensor').astype(jnp.float32)  68.6 us
    psum x1, waiting for transfers between devices, local(): lax.psum(normed_two_part.astype(jnp.bfloat16), 'tensor').astype(jnp.float32)  66.7 us
    unnamed x19, waiting for transfers between devices  38.1 us
    unnamed x135, local copies, waits for them, and re-layouts  37.6 us
    psum x1, waiting for transfers between devices, local(): lax.psum(gradients[1].astype(jnp.bfloat16), 'ctx').astype(jnp.float32)  36.4 us
    reduce_scatter x1, waiting for transfers between devices, local(): lax.psum_scatter(branch_part.astype(jnp.bfloat16), 'tensor', scatter_dime...  35.8 us
    all_gather x1, waiting for transfers between devices, local(): lax.all_gather(hidden_share.astype(jnp.bfloat16), 'tensor', axis=0, tiled...  34.9 us
    reduce_scatter x1, waiting for transfers between devices, local(): lax.psum_scatter(attn_part.astype(jnp.bfloat16), 'tensor', scatter_dimens...  34.8 us
  transfers between devices with their start and end apart: 15, of which 15 were waited for; matrix products, arithmetic and copies ran while one was open for 9% of the time, Pallas kernels for 0%

commit v1 on v0

v1 whole, which is shorter than its diff:
```python
import functools

import jax
import jax.numpy as jnp
from jax import lax
from jax.experimental import pallas as pl
from jax.experimental.pallas import tpu as pltpu
from jax.sharding import PartitionSpec as P

HD = 64
CTX = 4
TENSOR = 4
EPSILON = 1e-05
ROPE_BASE = 160000.0
MASKED = -1e30
LOG2E = 1.4426950408889634
NN = (((1,), (0,)), ((), ()))
NT = (((1,), (1,)), ((), ()))
TN = (((0,), (0,)), ((), ()))


def mm(a, b, dims=NN):
    return lax.dot_general(a, b, dims, preferred_element_type=jnp.float32)


def fwd_body(blocks, first, last, *refs):
    q_ref, mq_ref = refs[:2]
    kv_refs, mk_refs = refs[2 : 2 + blocks], refs[2 + blocks : 2 + 2 * blocks]
    rest = refs[2 + 2 * blocks :]
    rows = q_ref.shape[2]
    qb = min(rows, 512)
    if not first:
        m_in, acc_in, *rest = rest
    if last:
        out_ref, lse_ref, *rest = rest
    m_ref, acc_ref = rest
    if first:
        m_ref[...] = jnp.full_like(m_ref, MASKED)
        acc_ref[...] = jnp.zeros_like(acc_ref)
    else:
        m_ref[...] = m_in[...]
        acc_ref[...] = acc_in[...]
    for kv_ref, mk_ref in zip(kv_refs, mk_refs):
        keys = jnp.concatenate([kv_ref[0, :HD], mk_ref[...]], axis=0).T
        vals = jnp.concatenate([kv_ref[0, HD:], jnp.ones((16, rows), jnp.bfloat16)], axis=0)
        for j in range(rows // qb):
            at = slice(j * qb, (j + 1) * qb)
            right = jnp.concatenate([q_ref[0, :, at], mq_ref[:, at]], axis=0)
            s = mm(keys, right)
            old = m_ref[0, :, at]
            new = jnp.maximum(old, jnp.max(s, axis=0, keepdims=True))
            p = jnp.exp2(s - new).astype(jnp.bfloat16)
            acc_ref[0, :, at] = acc_ref[0, :, at] * jnp.exp2(old - new) + mm(vals, p)
            m_ref[0, :, at] = new
    if last:
        total = acc_ref[0, HD : HD + 1]
        out_ref[0] = acc_ref[0, :HD] / total
        lse_ref[0] = m_ref[0] + jnp.log2(total)


def per_head(a, b):
    return pl.BlockSpec((1, a, b), lambda h: (h, 0, 0))


def same(a, b):
    return pl.BlockSpec((a, b), lambda h: (0, 0))


def cost(heads, rows, keys, products):
    return pl.CostEstimate(
        flops=heads * rows * keys * HD * products * 8,
        bytes_accessed=4 * 2**20,
        transcendentals=heads * rows * keys,
    )


def attn_fwd(q, mq, kv, mk, state=None, last=False):
    heads, _, rows = q.shape
    blocks = len(kv)
    carried = [per_head(1, rows), per_head(HD + 16, rows)]
    result = [per_head(HD, rows), per_head(1, rows)]
    shape = lambda a: jax.ShapeDtypeStruct((heads, a, rows), jnp.float32)
    first = state is None
    return pl.pallas_call(
        functools.partial(fwd_body, blocks, first, last),
        grid=(heads,),
        in_specs=[per_head(HD, rows), same(HD, rows)]
        + [per_head(2 * HD, rows)] * blocks
        + [same(HD, rows)] * blocks
        + ([] if first else carried),
        out_specs=result if last else carried,
        out_shape=[shape(HD), shape(1)] if last else [shape(1), shape(HD + 16)],
        scratch_shapes=[]
        if not last
        else [pltpu.VMEM((1, 1, rows), jnp.float32), pltpu.VMEM((1, HD + 16, rows), jnp.float32)],
        compiler_params=pltpu.CompilerParams(vmem_limit_bytes=40 * 2**20),
        cost_estimate=cost(heads, rows, rows * blocks, 2),
        name="attend",
    )(q, mq, *kv, *mk, *(() if first else state))


def bwd_body(blocks, more, *refs):
    q_ref, mq_ref = refs[:2]
    kv_refs, mk_refs = refs[2 : 2 + blocks], refs[2 + blocks : 2 + 2 * blocks]
    lse_ref, do_ref, dl_ref, *rest = refs[2 + 2 * blocks :]
    if more:
        dq_in, dq_ref, *dkv_refs = rest
        dq_ref[...] = dq_in[...]
    else:
        dq_ref, *dkv_refs = rest
        dq_ref[...] = jnp.zeros_like(dq_ref)
    rows = q_ref.shape[2]
    qb = min(rows, 512)
    for kv_ref, mk_ref, dkv_ref in zip(kv_refs, mk_refs, dkv_refs):
        kt = kv_ref[0, :HD]
        keys = jnp.concatenate([kt, mk_ref[...]], axis=0).T
        vals = kv_ref[0, HD:].T
        dk = jnp.zeros((HD, rows), jnp.float32)
        dv = jnp.zeros((HD, rows), jnp.float32)
        for j in range(rows // qb):
            at = slice(j * qb, (j + 1) * qb)
            qj = q_ref[0, :, at]
            doj = do_ref[0, :, at]
            s = mm(keys, jnp.concatenate([qj, mq_ref[:, at]], axis=0))
            p = jnp.exp2(s - lse_ref[0, :, at])
            dp = mm(vals, doj)
            ds = (p * (dp - dl_ref[0, :, at])).astype(jnp.bfloat16)
            dv = dv + mm(doj, p.astype(jnp.bfloat16), NT)
            dk = dk + mm(qj, ds, NT)
            dq_ref[0, :, at] += mm(kt, ds)
        dkv_ref[0, :HD] = (dk * (1.0 / LOG2E)).astype(jnp.bfloat16)
        dkv_ref[0, HD:] = dv.astype(jnp.bfloat16)


def attn_bwd(q, mq, kv, mk, lse, do, delta, dq=None):
    heads, _, rows = q.shape
    blocks = len(kv)
    more = dq is not None
    out = pl.pallas_call(
        functools.partial(bwd_body, blocks, more),
        grid=(heads,),
        in_specs=[per_head(HD, rows), same(HD, rows)]
        + [per_head(2 * HD, rows)] * blocks
        + [same(HD, rows)] * blocks
        + [per_head(1, rows), per_head(HD, rows), per_head(1, rows)]
        + ([per_head(HD, rows)] if more else []),
        out_specs=[per_head(HD, rows)] + [per_head(2 * HD, rows)] * blocks,
        out_shape=[jax.ShapeDtypeStruct((heads, HD, rows), jnp.float32)]
        + [jax.ShapeDtypeStruct((heads, 2 * HD, rows), jnp.bfloat16)] * blocks,
        compiler_params=pltpu.CompilerParams(vmem_limit_bytes=40 * 2**20),
        cost_estimate=cost(heads, rows, rows * blocks, 5),
        name="attend_back",
    )(q, mq, *kv, *mk, lse, do, delta, *((dq,) if more else ()))
    return out[0], out[1:]


def swap(x, axis, size, d):
    return lax.ppermute(x, axis, [(i, i ^ d) for i in range(size)])


def norm_parts(values):
    centre = values - jnp.mean(values, axis=-1, keepdims=True)
    spread = jnp.mean(centre * centre, axis=-1, keepdims=True)
    scaling = lax.rsqrt(spread + EPSILON)
    return centre * scaling, scaling


def norm_back(scaled, normal, scaling):
    return scaling * (
        scaled
        - jnp.mean(scaled, axis=-1, keepdims=True)
        - normal * jnp.mean(scaled * normal, axis=-1, keepdims=True)
    )


def low(x):
    return x.astype(jnp.bfloat16)


def wide(x):
    return x.astype(jnp.float32)


def together(*values):
    return lax.optimization_barrier(values)


def local(dp, tokens, lengths, gain_attn, w_qkv, w_out, gain_mlp, w_in, w_down, cotangent):
    share, width = tokens.shape
    group = w_out.shape[0]
    heads = group // HD
    units = w_down.shape[0]
    half = w_out.shape[1]
    rows = share * TENSOR
    ctx = lax.axis_index("ctx")
    tensor = lax.axis_index("tensor")
    dp_index = lax.axis_index("dp")
    core, chip = ctx % 2, ctx // 2

    def gather_dp(x):
        if dp != 2:
            return lax.all_gather(x, "dp", axis=x.ndim - 1, tiled=True)
        other = swap(x, "dp", 2, 1)
        first = dp_index == 0
        return jnp.concatenate([jnp.where(first, x, other), jnp.where(first, other, x)], -1)

    def sum_dp(x):
        if dp != 2:
            return wide(lax.psum_scatter(low(x), "dp", scatter_dimension=x.ndim - 1, tiled=True))
        mine = lax.dynamic_slice_in_dim(x, dp_index * half, half, x.ndim - 1)
        theirs = lax.dynamic_slice_in_dim(x, (1 - dp_index) * half, half, x.ndim - 1)
        return wide(mine) + wide(swap(low(theirs), "dp", 2, 1))

    def over_z(x):
        return [x] + [swap(x, "tensor", TENSOR, d) for d in (1, 2, 3)]

    def pair_gather(x, bit, d, axis):
        other = swap(x, "ctx", CTX, d)
        return jnp.concatenate(
            [jnp.where(bit == 0, x, other), jnp.where(bit == 0, other, x)], axis
        )

    def pair_sum(x, bit, d, axis):
        mine = lax.dynamic_index_in_dim(x, bit, axis, False)
        theirs = lax.dynamic_index_in_dim(x, 1 - bit, axis, False)
        return wide(mine) + wide(swap(low(theirs), "ctx", CTX, d))

    def by_chip(x):
        return pair_gather(x[:, None], chip, 2, 1)

    def by_core(x):
        n, _, r, w = x.shape
        return pair_gather(x[:, :, None], core, 1, 2).reshape(n, CTX, r, w)

    def quarter(x):
        r = x.shape[-2] // 4
        return lax.dynamic_slice_in_dim(x, ctx * r, r, x.ndim - 2)

    token_parts = over_z(tokens)
    qkv_shard = jnp.swapaxes(w_qkv, 1, 2).reshape(3 * group, half)
    packed = jnp.concatenate([qkv_shard, gain_attn[None], gain_mlp[None]], 0)
    packed = gather_dp(packed)
    qkv_own = packed[: 3 * group]
    gain_one, gain_two = wide(packed[3 * group]), wide(packed[3 * group + 1])
    inputs = wide(tokens)

    g, n = group // CTX, units // CTX
    in_turned = jnp.swapaxes(w_in, 1, 2)
    quarters = [quarter(w_out), quarter(in_turned[0]), quarter(in_turned[1]), quarter(w_down)]
    quarters = jnp.concatenate(quarters, 0)

    normed_parts = []
    for part in token_parts:
        normal, _ = norm_parts(wide(part))
        normed_parts.append(low(normal * gain_one))
    quarters, *normed_parts = together(quarters, *normed_parts)
    weights = over_z(quarters)
    normed = jnp.concatenate(normed_parts, 0)
    project = jnp.concatenate([mm(qkv_own, part, NT) for part in normed_parts], 1)
    project = project.reshape(3, heads, HD, rows)

    block = jnp.arange(rows, dtype=jnp.int32) // share
    place = (block ^ tensor) * share + jnp.arange(rows, dtype=jnp.int32) % share
    bounds = jnp.cumsum(lengths[0])

    def segments(e):
        at = (ctx ^ e) * rows + place
        return jnp.sum((at[None, :] >= bounds[:, None]).astype(jnp.int32), axis=0)

    feature = lax.broadcasted_iota(jnp.int32, (HD, rows), 0)

    def key_mask(e):
        return (feature == segments(e)[None, :]).astype(jnp.bfloat16)

    query_mask = jnp.where(
        (feature == segments(0)[None, :]) | (feature >= lengths.shape[1]), 0.0, MASKED
    ).astype(jnp.bfloat16)
    exponent = jnp.arange(HD // 2, dtype=jnp.float32) * (2.0 / HD)
    angles = (ROPE_BASE ** (-exponent))[:, None] * (ctx * rows + place).astype(jnp.float32)[None, :]
    cosine, sine = jnp.cos(angles), jnp.sin(angles)

    def rotate(x, sine):
        a, b = x[:, : HD // 2], x[:, HD // 2 :]
        return jnp.concatenate([a * cosine - b * sine, b * cosine + a * sine], 1)

    queries = low(rotate(project[0], sine) * (HD**-0.5 * LOG2E))
    kv = jnp.concatenate([low(rotate(project[1], sine)), low(project[2])], 1)
    kv_core = swap(kv, "ctx", CTX, 1)
    kv_chip = swap(kv, "ctx", CTX, 2)

    ask = (queries, query_mask)
    state = attn_fwd(*ask, [kv], [key_mask(0)])
    *state, kv_core = together(*state, kv_core)
    state = attn_fwd(*ask, [kv_core], [key_mask(1)], state=state)
    *state, weights[1], weights[2], weights[3], kv_chip = together(*state, *weights[1:], kv_chip)
    weights_a = gather_dp(jnp.stack(weights[:2]))
    weights_b = by_chip(jnp.stack(weights[2:]))
    qkv_full = over_z(together(quarter(qkv_own), state[0])[0])
    kv_far = swap(kv_chip, "ctx", CTX, 1)
    far = ([kv_chip, kv_far], [key_mask(2), key_mask(3)])
    heads_out, logsum = attn_fwd(*ask, *far, state=state, last=True)
    heads_out, logsum, weights_a, weights_b, *qkv_full = together(
        heads_out, logsum, weights_a, weights_b, *qkv_full
    )
    heads_low = low(heads_out).reshape(group, rows)
    heads_own = jnp.concatenate(
        [heads_low[:, :share]]
        + [
            swap(heads_low[:, d * share : (d + 1) * share], "tensor", TENSOR, d)
            for d in (1, 2, 3)
        ],
        0,
    )

    weights_a = by_core(by_chip(weights_a))
    weights_b = by_core(gather_dp(weights_b))
    weights = jnp.concatenate([weights_a, weights_b], 0)
    out_full = weights[:, :, :g].reshape(-1, width)
    in_full = [weights[:, :, g + t * n : g + (t + 1) * n].reshape(-1, width) for t in (0, 1)]
    down_full = weights[:, :, g + 2 * n :].reshape(-1, width)
    heads_own, out_full, *in_full, down_full = together(heads_own, out_full, *in_full, down_full)
    qkv_full = by_chip(jnp.stack(qkv_full))
    hidden = inputs + mm(heads_own, out_full, TN)
    normal_two, scaling_two = norm_parts(hidden)
    normed_two = low(normal_two * gain_two)
    inner = [mm(in_full[t], normed_two, NT) for t in (0, 1)]
    activated, gelu_back = jax.vjp(lambda v: jax.nn.gelu(v, approximate=False), inner[0])
    product = low(activated * inner[1])
    grad_product = mm(down_full, cotangent, NT)
    grad_inner = [
        low(gelu_back(grad_product * inner[1])[0]),
        low(grad_product * activated),
    ]
    grad_normed_two = sum(mm(grad_inner[t], in_full[t], TN) for t in (0, 1))
    grad_hidden = wide(cotangent) + norm_back(grad_normed_two * gain_two, normal_two, scaling_two)
    grad_hidden_low = low(grad_hidden)
    grad_heads_own = low(mm(out_full, grad_hidden_low, NT))
    grad_heads_own, qkv_full = together(grad_heads_own, qkv_full)
    grad_heads_own = grad_heads_own.reshape(TENSOR, group, share)
    grad_heads = [grad_heads_own[0]] + [
        swap(grad_heads_own[d], "tensor", TENSOR, d) for d in (1, 2, 3)
    ]

    gain_sum = low(jnp.sum(grad_normed_two * normal_two, axis=0))
    gain_sum = jnp.broadcast_to(gain_sum, (TENSOR, 2, 8, width))

    def gradients(bit):
        def rows_of(x):
            x = x.reshape(TENSOR, 2, 2, -1, share)
            return lax.dynamic_index_in_dim(x, bit, 2, False).reshape(-1, share)

        def against(x, y):
            return low(mm(rows_of(x), y)).reshape(TENSOR, 2, -1, width)

        return jnp.concatenate(
            [
                against(heads_own, grad_hidden_low),
                against(grad_inner[0], normed_two),
                against(grad_inner[1], normed_two),
                against(product, cotangent),
                gain_sum,
            ],
            2,
        )

    theirs = swap(gradients(1 - core), "ctx", CTX, 1)
    grad_all = low(wide(gradients(core)) + wide(theirs))
    *grad_heads, grad_all = together(*grad_heads, grad_all)
    grad_heads = jnp.concatenate(grad_heads, 1).reshape(heads, HD, rows)
    part_a = pair_sum(grad_all[:2], chip, 2, 1)
    part_b = sum_dp(grad_all[2:])

    delta = jnp.sum(wide(grad_heads) * heads_out, axis=1, keepdims=True)
    given = (logsum, grad_heads, delta)
    grad_q, (grad_chip, grad_far) = attn_bwd(*ask, *far, *given)
    grad_q, grad_chip, grad_far, part_a, part_b = together(
        grad_q, grad_chip, grad_far, part_a, part_b
    )
    from_core = swap(grad_far, "ctx", CTX, 1)
    from_chip = swap(low(wide(grad_chip) + wide(from_core)), "ctx", CTX, 2)
    part_a = sum_dp(part_a)
    part_b = pair_sum(part_b, chip, 2, 1)
    grad_q, (grad_core,) = attn_bwd(*ask, [kv_core], [key_mask(1)], *given, dq=grad_q)
    grad_q, grad_core, part_a, part_b = together(grad_q, grad_core, part_a, part_b)
    parts = [part_a[0], low(part_a[1]), low(part_b[0]), low(part_b[1])]
    parts[1:] = [swap(parts[d], "tensor", TENSOR, d) for d in (1, 2, 3)]
    from_pair = swap(grad_core, "ctx", CTX, 1)
    grad_q, (grad_kv,) = attn_bwd(*ask, [kv], [key_mask(0)], *given, dq=grad_q)
    grad_q, grad_kv, from_pair, from_chip = together(grad_q, grad_kv, from_pair, from_chip)
    grad_kv = wide(grad_kv) + wide(from_pair) + wide(from_chip)
    grad_project = jnp.stack(
        [
            low(rotate(grad_q * HD**-0.5, -sine)),
            low(rotate(grad_kv[:, :HD], -sine)),
            low(grad_kv[:, HD:]),
        ]
    ).reshape(3 * group, rows)
    grad_project, *parts = together(grad_project, *parts)
    own_project = jnp.concatenate(
        [grad_project[:, :share]]
        + [
            swap(grad_project[:, d * share : (d + 1) * share], "tensor", TENSOR, d)
            for d in (1, 2, 3)
        ],
        0,
    )
    qkv_full = by_core(qkv_full).reshape(-1, width)
    grad_normed = mm(own_project, qkv_full, TN)
    normal_one, scaling_one = norm_parts(inputs)
    grad_inputs = grad_hidden + norm_back(grad_normed * gain_one, normal_one, scaling_one)
    grad_tokens = low(grad_inputs)

    grad_qkv = low(mm(grad_project, normed)).reshape(2, 2, -1, width)
    grad_qkv = sum_dp(pair_sum(low(pair_sum(grad_qkv, core, 1, 1)), chip, 2, 0))
    gain_sum = jnp.sum(grad_qkv * wide(quarter(qkv_shard)), axis=0, keepdims=True)
    gain_sum = sum(over_z(gain_sum))
    grad_qkv = jnp.concatenate([grad_qkv, jnp.broadcast_to(gain_sum, (16, half))], 0)
    grad_qkv = wide(by_core(by_chip(low(grad_qkv)[None])))[0]
    grad_gain_attn = jnp.sum(grad_qkv[:, -1], axis=0) / wide(gain_attn)
    grad_qkv = grad_qkv[:, :-16].reshape(3, group, half)

    grad_all = sum(wide(p) for p in parts)
    grad_all = wide(by_core(by_chip(low(grad_all)[None])))[0]
    grad_out = grad_all[:, :g].reshape(group, half)
    grad_in = jnp.stack(
        [grad_all[:, g + t * n : g + (t + 1) * n].reshape(units, half) for t in (0, 1)]
    )
    grad_down = grad_all[:, g + 2 * n : g + 3 * n].reshape(units, half)
    grad_gain_mlp = grad_all[0, g + 3 * n]
    activations = low(hidden + mm(product, down_full, TN))

    return (
        activations,
        grad_tokens,
        grad_gain_attn,
        wide(jnp.swapaxes(grad_qkv, 1, 2)),
        grad_out,
        grad_gain_mlp,
        jnp.swapaxes(grad_in, 1, 2),
        grad_down,
    )


def solution(mesh):
    rows = P(("dp", "ctx", "tensor"), None)
    weights = (P(None, "dp", "tensor"), P("tensor", "dp"))
    return jax.shard_map(
        functools.partial(local, mesh.shape["dp"]),
        mesh=mesh,
        in_specs=(rows, P("dp", None), P("dp"), *weights, P("dp"), *weights, rows),
        out_specs=(rows, rows, P("dp"), *weights, P("dp"), *weights),
        check_vma=False,
    )
```

time: 754 us -> 297 us (0.39)
  waiting for transfers between devices: 389 us -> 90.9 us
  matrix products: 141 us -> 18.5 us
  Pallas kernels: 0 us -> 57.3 us
  blocking collectives: 55.6 us -> 0 us
  starting transfers between devices: 9.65 us -> 63.1 us
  other arithmetic: 72.8 us -> 36.7 us
  local copies, waits for them, and re-layouts: 58.1 us -> 22.8 us
  between operations: 15.6 us -> 2.48 us
    psum x3 -> x0, waiting for transfers between devices: 172 us -> none  [the longest x1 68.6 us: local(): lax.psum(normed_part.astype(jnp.bfloat16), 'tensor').astype(jnp.float32)]
    dot_general x67 -> x22, matrix products: 140 us -> 18.5 us  [mm(): return lax.dot_general(a, b, dims, preferred_element_type=jnp.float32)]
    all_gather x5 -> x0, waiting for transfers between devices: 100 us -> none  [the longest x1 34.9 us: local(): lax.all_gather(hidden_share.astype(jnp.bfloat16), 'tensor', axis=0, tiled...]
    ppermute x0 -> x51, waiting for transfers between devices: none -> 90.9 us  [swap(): return lax.ppermute(x, axis, [(i, i ^ d) for i in range(size)])]
    reduce_scatter x3 -> x0, waiting for transfers between devices: 79.3 us -> none  [the longest x1 35.8 us: local(): lax.psum_scatter(branch_part.astype(jnp.bfloat16), 'tensor', scatter_dime...]
    ppermute x0 -> x51, starting transfers between devices: none -> 63.1 us  [swap(): return lax.ppermute(x, axis, [(i, i ^ d) for i in range(size)])]
    pallas_call x0 -> x6, Pallas kernels: none -> 57.3 us  [the longest x3 34.2 us: attn_bwd(): pl.pallas_call(functools.partial(bwd_body, blocks, more), grid=(heads,),...]
    all_gather x6 -> x0, blocking collectives: 44.6 us -> none  [the longest x1 12 us: local(): lax.all_gather(w_qkv, 'dp', axis=1, tiled=True)]
  transfers between devices with their start and end apart: 15 -> 51, of which waited for: 15 -> 22; matrix products, arithmetic and copies ran while one was open for 9% -> 20% of each run, Pallas kernels for 0% -> 20%
where the time goes in v1:
time: 297 us; the launch traced here: 292 us
  waiting for transfers between devices  90.9 us (31%)
  starting transfers between devices  63.1 us (21%)
  Pallas kernels  57.3 us (19%)
  other arithmetic  36.7 us (12%)
  local copies, waits for them, and re-layouts  22.8 us (8%)
  matrix products  18.5 us (6%)
    ppermute x51, waiting for transfers between devices, swap(): return lax.ppermute(x, axis, [(i, i ^ d) for i in range(size)])  90.9 us
    ppermute x51, starting transfers between devices, swap(): return lax.ppermute(x, axis, [(i, i ^ d) for i in range(size)])  63.1 us
    pallas_call x3, Pallas kernels, attn_bwd(): pl.pallas_call(functools.partial(bwd_body, blocks, more), grid=(heads,),...  34.2 us
    pallas_call x3, Pallas kernels, attn_fwd(): pl.pallas_call(functools.partial(fwd_body, blocks, first, last), grid=(he...  23.1 us
    dot_general x22, matrix products, mm(): return lax.dot_general(a, b, dims, preferred_element_type=jnp.float32)  18.5 us
    unnamed x110, local copies, waits for them, and re-layouts  12.4 us
    select_n x10, other arithmetic, pair_gather(): jnp.where(bit == 0, x, other)  6.99 us
    convert_element_type x8, other arithmetic, low(): return x.astype(jnp.bfloat16)  6.34 us
  transfers between devices with their start and end apart: 51, of which 22 were waited for; matrix products, arithmetic and copies ran while one was open for 20% of the time, Pallas kernels for 20%

profile of v1, /device:TPU:0, one launch (start us, length us, event | category | flops | bytes accessed | tf_op | source)
XLA Modules:
  0.0 291.7 jit_solution(3496102802533374611)
XLA Ops:
  0.7 5.1 %collective-permute-start.3 = (bf16[256,768]{1,0:T(8,128)(2,1)}, bf16[256,768]{1,0:T(8,128)(2,1)S(1)}, u32[]{:S(2)}, u32[]{:S(2)}) collective-permute-start(bf16[256,768]{1,0:T(8,128)(2,1)} %param.9), channel_id=1, source_target_pairs={{0,3},{1,2},{2,1},{3,0},{4,7},{5,6},{6,5},{7,4},{8,11},{9,10},{10,... | collective-permute-start | bytes 1179656 | tf_op jit(solution)/shard_map/ppermute | solution.py:158
  8.9 1.7 collective-permute-start
  16.8 7.9 %collective-permute-done.1 = bf16[256,768]{1,0:T(8,128)(2,1)S(1)} collective-permute-done((bf16[256,768]{1,0:T(8,128)(2,1)}, bf16[256,768]{1,0:T(8,128)(2,1)S(1)}, u32[]{:S(2)}, u32[]{:S(2)}) %collective-permute-start.1) | collective-permute-done | bytes 393248 | tf_op jit(solution)/shard_map/ppermute | solution.py:158
  24.8 14.7 %collective-permute-done.2 = bf16[256,768]{1,0:T(8,128)(2,1)S(1)} collective-permute-done((bf16[256,768]{1,0:T(8,128)(2,1)}, bf16[256,768]{1,0:T(8,128)(2,1)S(1)}, u32[]{:S(2)}, u32[]{:S(2)}) %collective-permute-start.2) | collective-permute-done | bytes 393248 | tf_op jit(solution)/shard_map/ppermute | solution.py:158
  46.7 1.6 collective-permute-start.8
  48.4 3.0 %collective-permute-start.6 = (bf16[264,384]{1,0:T(8,128)(2,1)}, bf16[264,384]{1,0:T(8,128)(2,1)S(1)}, u32[]{:S(2)}, u32[]{:S(2)}) collective-permute-start(bf16[264,384]{1,0:T(8,128)(2,1)} %pad_maximum_fusion.19), channel_id=1, source_target_pairs={{0,2},{1,3},{2,0},{3,1},{4,6},{5,7},{6,4},{7,5},{8,10},{9,11},{10,... | collective-permute-start | bytes 608264 | tf_op jit(solution)/shard_map/ppermute | solution.py:158
  54.0 6.0 %attend.3 = (f32[3,1,1024]{2,1,0:T(1,128)S(1)}, f32[3,80,1024]{2,1,0:T(8,128)S(1)}) custom-call(bf16[3,64,1024]{2,1,0:T(8,128)(2,1)S(1)} %fusion.54.refs_0_, bf16[64,1024]{1,0:T(8,128)(2,1)S(1)} %select_convert_fusion.refs_1_, bf16[3,128,1024]{2,1,0:T(8,128)(2,1)S(1)} %pad_maximum_fusion.14.refs_2_, bf16[64,1024]{1,0:T(8,128)(2,1)S(1)} %fusion.57.refs_3_), custom_call_target="tpu_custom_call" | custom-call | flops 3221225472 | bytes 4194304 | tf_op jit(solution)/shard_map/attend/pallas_call | solution.py:84
  60.0 5.9 %attend.4 = (f32[3,1,1024]{2,1,0:T(1,128)S(1)}, f32[3,80,1024]{2,1,0:T(8,128)S(1)}) custom-call(bf16[3,64,1024]{2,1,0:T(8,128)(2,1)S(1)} %fusion.54.refs_0_, bf16[64,1024]{1,0:T(8,128)(2,1)S(1)} %select_convert_fusion.refs_1_, bf16[3,128,1024]{2,1,0:T(8,128)(2,1)S(1)} %collective-permute-done.4.refs_2_, bf16[64,1024]{1,0:T(8,128)(2,1)S(1)} %fusion.59.refs_3_, ...), custom_call_target="tpu_custom_call" | custom-call | flops 3221225472 | bytes 4194304 | tf_op jit(solution)/shard_map/attend/pallas_call | solution.py:84
  67.9 1.6 collective-permute-start.10
  69.7 1.6 collective-permute-start.11
  72.2 2.8 collective-permute-start.12
  76.0 3.0 %collective-permute-done.10 = bf16[2,264,384]{2,1,0:T(8,128)(2,1)S(1)} collective-permute-done((bf16[2,264,384]{2,1,0:T(8,128)(2,1)S(1)}, bf16[2,264,384]{2,1,0:T(8,128)(2,1)S(1)}, u32[]{:S(2)}, u32[]{:S(2)}) %collective-permute-start.10) | collective-permute-done | bytes 405536 | tf_op jit(solution)/shard_map/ppermute | solution.py:158
  79.0 2.5 collective-permute-start.14
  83.7 11.2 %attend.5 = (f32[3,64,1024]{2,1,0:T(8,128)S(1)}, f32[3,1,1024]{2,1,0:T(1,128)S(1)}) custom-call(bf16[3,64,1024]{2,1,0:T(8,128)(2,1)S(1)} %fusion.54.refs_0_, bf16[64,1024]{1,0:T(8,128)(2,1)S(1)} %select_convert_fusion.refs_1_, bf16[3,128,1024]{2,1,0:T(8,128)(2,1)S(1)} %copy-done.3, bf16[3,128,1024]{2,1,0:T(8,128)(2,1)S(1)} %collective-permute-done.9.refs_3_, ...), custom_call_target="tpu_custom_call" | custom-call | flops 6442450944 | bytes 4194304 | tf_op jit(solution)/shard_map/attend/pallas_call | solution.py:84
  95.0 1.6 collective-permute-start.20
  98.1 15.5 %collective-permute-done.20 = bf16[2,2,264,384]{3,2,1,0:T(8,128)(2,1)S(1)} collective-permute-done((bf16[2,2,264,384]{3,2,1,0:T(8,128)(2,1)S(1)}, bf16[2,2,264,384]{3,2,1,0:T(8,128)(2,1)S(1)}, u32[]{:S(2)}, u32[]{:S(2)}) %collective-permute-start.20) | collective-permute-done | bytes 811040 | tf_op jit(solution)/shard_map/ppermute | solution.py:158
  117.9 1.7 collective-permute-start.17
  119.6 3.7 %collective-permute-start.16 = (bf16[192,256]{1,0:T(8,128)(2,1)S(1)}, bf16[192,256]{1,0:T(8,128)(2,1)S(1)}, u32[]{:S(2)}, u32[]{:S(2)}) collective-permute-start(bf16[192,256]{1,0:T(8,128)(2,1)S(1)} %get-tuple-element.221), channel_id=1, source_target_pairs={{0,2},{1,3},{2,0},{3,1},{4,6},{5,7},{6,4},{7,5},{8,10},{9,11},{10,... | collective-permute-start | bytes 294920 | tf_op jit(solution)/shard_map/ppermute | solution.py:158
  124.5 1.6 collective-permute-start.22
  126.1 4.7 %collective-permute-done.16 = bf16[192,256]{1,0:T(8,128)(2,1)S(1)} collective-permute-done((bf16[192,256]{1,0:T(8,128)(2,1)S(1)}, bf16[192,256]{1,0:T(8,128)(2,1)S(1)}, u32[]{:S(2)}, u32[]{:S(2)}) %collective-permute-start.16) | collective-permute-done | bytes 98336 | tf_op jit(solution)/shard_map/ppermute | solution.py:158
  130.9 2.1 broadcast_select_fusion.3
  134.3 2.0 broadcast_select_fusion.5
  139.8 2.9 multiply_convert_fusion
  154.1 1.5 copy-done.23
  159.4 2.2 collective-permute-start.24
  161.6 2.2 collective-permute-start.25
  163.8 3.3 %fusion.11 = bf16[256,768]{1,0:T(8,128)(2,1)} fusion(f32[256,768]{1,0:T(8,128)} %copy-done.7, bf16[1152,256]{1,0:T(8,128)(2,1)} %copy-done.28, bf16[1152,768]{1,0:T(8,128)(2,1)} %bitcast.202), kind=kOutput, calls=%fused_computation.44 | convolution fusion | flops 453378048 | bytes 3538944 | tf_op jit(solution)/shard_map/dot_general | solution.py:23
  167.1 2.2 broadcast_select_fusion.1
  171.3 2.9 add_convert_fusion
  174.7 1.6 collective-permute-start.27
  176.4 1.6 collective-permute-start.28
  178.0 16.7 %attend_back.3 = (f32[3,64,1024]{2,1,0:T(8,128)S(1)}, bf16[3,128,1024]{2,1,0:T(8,128)(2,1)S(1)}, bf16[3,128,1024]{2,1,0:T(8,128)(2,1)S(1)}) custom-call(bf16[3,64,1024]{2,1,0:T(8,128)(2,1)S(1)} %fusion.54.refs_0_, bf16[64,1024]{1,0:T(8,128)(2,1)S(1)} %select_convert_fusion.refs_1_, bf16[3,128,1024]{2,1,0:T(8,128)(2,1)S(1)} %copy-done.4, ...), custom_call_target="tpu_custom_call" | custom-call | flops 16106127360 | bytes 4194304 | tf_op jit(solution)/shard_map/attend_back/pallas_call | solution.py:139
  196.6 1.6 collective-permute-start.29
  198.8 8.6 %attend_back.4 = (f32[3,64,1024]{2,1,0:T(8,128)S(1)}, bf16[3,128,1024]{2,1,0:T(8,128)(2,1)S(1)}) custom-call(bf16[3,64,1024]{2,1,0:T(8,128)(2,1)S(1)} %fusion.54.refs_0_, bf16[64,1024]{1,0:T(8,128)(2,1)S(1)} %select_convert_fusion.refs_1_, bf16[3,128,1024]{2,1,0:T(8,128)(2,1)S(1)} %collective-permute-done.4.refs_2_, bf16[64,1024]{1,0:T(8,128)(2,1)S(1)} %fusion.59.refs_3_, ...), custom_call_target="tpu_custom_call" | custom-call | flops 8053063680 | bytes 4194304 | tf_op jit(solution)/shard_map/attend_back/pallas_call | solution.py:139
  210.1 1.6 collective-permute-start.33
  212.3 2.5 collective-permute-start.36
  214.8 8.8 %attend_back.5 = (f32[3,64,1024]{2,1,0:T(8,128)S(1)}, bf16[3,128,1024]{2,1,0:T(8,128)(2,1)S(1)}) custom-call(bf16[3,64,1024]{2,1,0:T(8,128)(2,1)S(1)} %fusion.54.refs_0_, bf16[64,1024]{1,0:T(8,128)(2,1)S(1)} %select_convert_fusion.refs_1_, bf16[3,128,1024]{2,1,0:T(8,128)(2,1)S(1)} %pad_maximum_fusion.14.refs_2_, bf16[64,1024]{1,0:T(8,128)(2,1)S(1)} %fusion.57.refs_3_, ...), custom_call_target="tpu_custom_call" | custom-call | flops 8053063680 | bytes 4194304 | tf_op jit(solution)/shard_map/attend_back/pallas_call | solution.py:139
  223.7 6.1 %collective-permute-done.33 = bf16[3,128,1024]{2,1,0:T(8,128)(2,1)S(1)} collective-permute-done((bf16[3,128,1024]{2,1,0:T(8,128)(2,1)S(1)}, bf16[3,128,1024]{2,1,0:T(8,128)(2,1)S(1)}, u32[]{:S(2)}, u32[]{:S(2)}) %collective-permute-start.33) | collective-permute-done | bytes 786464 | tf_op jit(solution)/shard_map/ppermute | solution.py:158
  233.6 1.6 collective-permute-start.49
  237.1 2.6 collective-permute-start.37
  240.5 6.7 %collective-permute-done.39 = bf16[576,256]{1,0:T(8,128)(2,1)S(1)} collective-permute-done((bf16[576,256]{1,0:T(8,128)(2,1)S(1)}, bf16[576,256]{1,0:T(8,128)(2,1)S(1)}, u32[]{:S(2)}, u32[]{:S(2)}) %collective-permute-start.39) | collective-permute-done | bytes 294944 | tf_op jit(solution)/shard_map/ppermute | solution.py:158
  247.2 14.8 %collective-permute-done.38 = bf16[576,256]{1,0:T(8,128)(2,1)S(1)} collective-permute-done((bf16[576,256]{1,0:T(8,128)(2,1)S(1)}, bf16[576,256]{1,0:T(8,128)(2,1)S(1)}, u32[]{:S(2)}, u32[]{:S(2)}) %collective-permute-start.38) | collective-permute-done | bytes 294944 | tf_op jit(solution)/shard_map/ppermute | solution.py:158
  264.5 1.8 collective-permute-start.42
  266.4 4.6 %collective-permute-done.42 = bf16[144,768]{1,0:T(8,128)(2,1)S(1)} collective-permute-done((bf16[144,768]{1,0:T(8,128)(2,1)S(1)}, bf16[144,768]{1,0:T(8,128)(2,1)S(1)}, u32[]{:S(2)}, u32[]{:S(2)}) %collective-permute-start.42) | collective-permute-done | bytes 221216 | tf_op jit(solution)/shard_map/ppermute | solution.py:158
  271.3 4.6 %collective-permute-done.43 = bf16[144,384]{1,0:T(8,128)(2,1)S(1)} collective-permute-done((bf16[144,384]{1,0:T(8,128)(2,1)S(1)}, bf16[144,384]{1,0:T(8,128)(2,1)S(1)}, u32[]{:S(2)}, u32[]{:S(2)}) %collective-permute-start.43) | collective-permute-done | bytes 110624 | tf_op jit(solution)/shard_map/ppermute | solution.py:158
  278.0 3.4 %collective-permute-start.44 = (f32[1,384]{1,0:T(1,128)S(1)}, f32[1,384]{1,0:T(1,128)S(1)}, u32[]{:S(2)}, u32[]{:S(2)}) collective-permute-start(f32[1,384]{1,0:T(1,128)S(1)} %broadcast_in_dim.48), channel_id=1, source_target_pairs={{0,1},{1,0},{2,3},{3,2},{4,5},{5,4},{6,7},{7,6},{8,9},{9,8},{10,11... | collective-permute-start | bytes 4616 | tf_op jit(solution)/shard_map/ppermute | solution.py:158
  283.0 1.8 collective-permute-start.47
  286.4 1.6 collective-permute-done.47
  (331 shorter events, 78.1 us)
Async XLA Ops:
  0.7 15.7 %collective-permute-start.3 = (bf16[256,768]{1,0:T(8,128)(2,1)}, bf16[256,768]{1,0:T(8,128)(2,1)S(1)}, u32[]{:S(2)}, u32[]{:S(2)}) collective-permute-start(bf16[256,768]{1,0:T(8,128)(2,1)} %param.9), channel_id=1, source_target_pairs={{0,3},{1,2},{2,1},{3,0},{4,7},{5,6},{6,5},{7,4},{8,11},{9,10},{10,... | collective-permute-start | bytes 1179656 | tf_op jit(solution)/shard_map/ppermute | solution.py:158
  5.8 18.9 %collective-permute-start.1 = (bf16[256,768]{1,0:T(8,128)(2,1)}, bf16[256,768]{1,0:T(8,128)(2,1)S(1)}, u32[]{:S(2)}, u32[]{:S(2)}) collective-permute-start(bf16[256,768]{1,0:T(8,128)(2,1)} %param.9), channel_id=1, source_target_pairs={{0,1},{1,0},{2,3},{3,2},{4,5},{5,4},{6,7},{7,6},{8,9},{9,8},{10,11... | collective-permute-start | bytes 1179656 | tf_op jit(solution)/shard_map/ppermute | solution.py:158
  5.8 33.8 %collective-permute-start.2 = (bf16[256,768]{1,0:T(8,128)(2,1)}, bf16[256,768]{1,0:T(8,128)(2,1)S(1)}, u32[]{:S(2)}, u32[]{:S(2)}) collective-permute-start(bf16[256,768]{1,0:T(8,128)(2,1)} %param.9), channel_id=1, source_target_pairs={{0,2},{1,3},{2,0},{3,1},{4,6},{5,7},{6,4},{7,5},{8,10},{9,11},{10,... | collective-permute-start | bytes 1179656 | tf_op jit(solution)/shard_map/ppermute | solution.py:158
  8.9 31.3 %collective-permute-start = (bf16[578,384]{1,0:T(8,128)(2,1)S(1)}, bf16[578,384]{1,0:T(8,128)(2,1)}, u32[]{:S(2)}, u32[]{:S(2)}) collective-permute-start(bf16[578,384]{1,0:T(8,128)(2,1)S(1)} %pad_maximum_fusion.15), channel_id=1, source_target_pairs={{0,16},{16,0},{1,17},{17,1},{2,18},{18,2},{3,19},{19,3},{4,20},{20... | collective-permute-start | bytes 1331720 | tf_op jit(solution)/shard_map/ppermute | solution.py:158
  46.6 13.4 %collective-permute-start.4 = (bf16[3,128,1024]{2,1,0:T(8,128)(2,1)S(1)}, bf16[3,128,1024]{2,1,0:T(8,128)(2,1)S(1)}, u32[]{:S(2)}, u32[]{:S(2)}) collective-permute-start(bf16[3,128,1024]{2,1,0:T(8,128)(2,1)S(1)} %pad_maximum_fusion.14.refs_2_), channel_id=1, source_target_pairs={{0,4},{4,0},{8,12},{12,8},{1,5},{5,1},{9,13},{13,9},{2,6},{6,2},{1... | collective-permute-start | bytes 2359304 | tf_op jit(solution)/shard_map/ppermute | solution.py:158
  46.7 20.0 %collective-permute-start.8 = (bf16[3,128,1024]{2,1,0:T(8,128)(2,1)S(1)}, bf16[3,128,1024]{2,1,0:T(8,128)(2,1)S(1)}, u32[]{:S(2)}, u32[]{:S(2)}) collective-permute-start(bf16[3,128,1024]{2,1,0:T(8,128)(2,1)S(1)} %pad_maximum_fusion.14.refs_2_), channel_id=1, source_target_pairs={{0,8},{4,12},{8,0},{12,4},{1,9},{5,13},{9,1},{13,5},{2,10},{6,14},... | collective-permute-start | bytes 2359304 | tf_op jit(solution)/shard_map/ppermute | solution.py:158
  48.4 17.6 %collective-permute-start.5 = (bf16[264,384]{1,0:T(8,128)(2,1)}, bf16[264,384]{1,0:T(8,128)(2,1)S(1)}, u32[]{:S(2)}, u32[]{:S(2)}) collective-permute-start(bf16[264,384]{1,0:T(8,128)(2,1)} %pad_maximum_fusion.19), channel_id=1, source_target_pairs={{0,1},{1,0},{2,3},{3,2},{4,5},{5,4},{6,7},{7,6},{8,9},{9,8},{10,11... | collective-permute-start | bytes 608264 | tf_op jit(solution)/shard_map/ppermute | solution.py:158
  48.4 17.9 %collective-permute-start.6 = (bf16[264,384]{1,0:T(8,128)(2,1)}, bf16[264,384]{1,0:T(8,128)(2,1)S(1)}, u32[]{:S(2)}, u32[]{:S(2)}) collective-permute-start(bf16[264,384]{1,0:T(8,128)(2,1)} %pad_maximum_fusion.19), channel_id=1, source_target_pairs={{0,2},{1,3},{2,0},{3,1},{4,6},{5,7},{6,4},{7,5},{8,10},{9,11},{10,... | collective-permute-start | bytes 608264 | tf_op jit(solution)/shard_map/ppermute | solution.py:158
  51.5 14.8 %collective-permute-start.7 = (bf16[264,384]{1,0:T(8,128)(2,1)}, bf16[264,384]{1,0:T(8,128)(2,1)S(1)}, u32[]{:S(2)}, u32[]{:S(2)}) collective-permute-start(bf16[264,384]{1,0:T(8,128)(2,1)} %pad_maximum_fusion.19), channel_id=1, source_target_pairs={{0,3},{1,2},{2,1},{3,0},{4,7},{5,6},{6,5},{7,4},{8,11},{9,10},{10,... | collective-permute-start | bytes 608264 | tf_op jit(solution)/shard_map/ppermute | solution.py:158
  67.9 11.1 %collective-permute-start.10 = (bf16[2,264,384]{2,1,0:T(8,128)(2,1)S(1)}, bf16[2,264,384]{2,1,0:T(8,128)(2,1)S(1)}, u32[]{:S(2)}, u32[]{:S(2)}) collective-permute-start(bf16[2,264,384]{2,1,0:T(8,128)(2,1)S(1)} %pad_maximum_fusion.16), channel_id=1, source_target_pairs={{0,16},{16,0},{1,17},{17,1},{2,18},{18,2},{3,19},{19,3},{4,20},{20... | collective-permute-start | bytes 1216520 | tf_op jit(solution)/shard_map/ppermute | solution.py:158
  69.5 13.3 %collective-permute-start.9 = (bf16[3,128,1024]{2,1,0:T(8,128)(2,1)S(1)}, bf16[3,128,1024]{2,1,0:T(8,128)(2,1)S(1)}, u32[]{:S(2)}, u32[]{:S(2)}) collective-permute-start(bf16[3,128,1024]{2,1,0:T(8,128)(2,1)S(1)} %collective-permute-done.8.refs_2_), channel_id=1, source_target_pairs={{0,4},{4,0},{8,12},{12,8},{1,5},{5,1},{9,13},{13,9},{2,6},{6,2},{1... | collective-permute-start | bytes 2359304 | tf_op jit(solution)/shard_map/ppermute | solution.py:158
  69.7 13.0 %collective-permute-start.11 = (bf16[2,1,264,384]{3,2,1,0:T(8,128)(2,1)S(1)}, bf16[2,1,264,384]{3,2,1,0:T(8,128)(2,1)S(1)}, u32[]{:S(2)}, u32[]{:S(2)}) collective-permute-start(bf16[2,1,264,384]{3,2,1,0:T(8,128)(2,1)S(1)} %maximum_bitcast_fusion.4), channel_id=1, source_target_pairs={{0,8},{4,12},{8,0},{12,4},{1,9},{5,13},{9,1},{13,5},{2,10},{6,14},... | collective-permute-start | bytes 1216520 | tf_op jit(solution)/shard_map/ppermute | solution.py:158
  72.2 22.7 %collective-permute-start.12 = (bf16[144,768]{1,0:T(8,128)(2,1)S(1)}, bf16[144,768]{1,0:T(8,128)(2,1)S(1)}, u32[]{:S(2)}, u32[]{:S(2)}) collective-permute-start(bf16[144,768]{1,0:T(8,128)(2,1)S(1)} %constant_dynamic-slice_fusion.9), channel_id=1, source_target_pairs={{0,1},{1,0},{2,3},{3,2},{4,5},{5,4},{6,7},{7,6},{8,9},{9,8},{10,11... | collective-permute-start | bytes 663560 | tf_op jit(solution)/shard_map/ppermute | solution.py:158
  75.0 20.0 %collective-permute-start.13 = (bf16[144,768]{1,0:T(8,128)(2,1)S(1)}, bf16[144,768]{1,0:T(8,128)(2,1)S(1)}, u32[]{:S(2)}, u32[]{:S(2)}) collective-permute-start(bf16[144,768]{1,0:T(8,128)(2,1)S(1)} %constant_dynamic-slice_fusion.9), channel_id=1, source_target_pairs={{0,2},{1,3},{2,0},{3,1},{4,6},{5,7},{6,4},{7,5},{8,10},{9,11},{10,... | collective-permute-start | bytes 663560 | tf_op jit(solution)/shard_map/ppermute | solution.py:158
  79.0 16.0 %collective-permute-start.14 = (bf16[144,768]{1,0:T(8,128)(2,1)S(1)}, bf16[144,768]{1,0:T(8,128)(2,1)S(1)}, u32[]{:S(2)}, u32[]{:S(2)}) collective-permute-start(bf16[144,768]{1,0:T(8,128)(2,1)S(1)} %constant_dynamic-slice_fusion.9), channel_id=1, source_target_pairs={{0,3},{1,2},{2,1},{3,0},{4,7},{5,6},{6,5},{7,4},{8,11},{9,10},{10,... | collective-permute-start | bytes 663560 | tf_op jit(solution)/shard_map/ppermute | solution.py:158
  95.0 18.6 %collective-permute-start.20 = (bf16[2,2,264,384]{3,2,1,0:T(8,128)(2,1)S(1)}, bf16[2,2,264,384]{3,2,1,0:T(8,128)(2,1)S(1)}, u32[]{:S(2)}, u32[]{:S(2)}) collective-permute-start(bf16[2,2,264,384]{3,2,1,0:T(8,128)(2,1)S(1)} %pad_maximum_fusion.13), channel_id=1, source_target_pairs={{0,16},{16,0},{1,17},{17,1},{2,18},{18,2},{3,19},{19,3},{4,20},{20... | collective-permute-start | bytes 2433032 | tf_op jit(solution)/shard_map/ppermute | solution.py:158
  96.6 18.9 %collective-permute-start.18 = (bf16[2,1,264,768]{3,2,0,1:T(8,128)(2,1)S(1)}, bf16[2,1,264,768]{3,2,0,1:T(8,128)(2,1)S(1)}, u32[]{:S(2)}, u32[]{:S(2)}) collective-permute-start(bf16[2,1,264,768]{3,2,0,1:T(8,128)(2,1)S(1)} %bitcast.217), channel_id=1, source_target_pairs={{0,8},{4,12},{8,0},{12,4},{1,9},{5,13},{9,1},{13,5},{2,10},{6,14},... | collective-permute-start | bytes 2433032 | tf_op jit(solution)/shard_map/ppermute | solution.py:158
  115.5 15.4 %collective-permute-start.21 = (bf16[2,2,1,264,768]{4,3,2,1,0:T(8,128)(2,1)}, bf16[2,2,1,264,768]{4,3,2,1,0:T(8,128)(2,1)}, u32[]{:S(2)}, u32[]{:S(2)}) collective-permute-start(bf16[2,2,1,264,768]{4,3,2,1,0:T(8,128)(2,1)} %maximum_bitcast_fusion), channel_id=1, source_target_pairs={{0,4},{4,0},{8,12},{12,8},{1,5},{5,1},{9,13},{13,9},{2,6},{6,2},{1... | collective-permute-start | bytes 4866056 | tf_op jit(solution)/shard_map/ppermute | solution.py:158
  117.3 16.0 %collective-permute-start.19 = (bf16[2,2,1,264,768]{4,3,2,1,0:T(8,128)(2,1)}, bf16[2,2,1,264,768]{4,3,2,1,0:T(8,128)(2,1)}, u32[]{:S(2)}, u32[]{:S(2)}) collective-permute-start(bf16[2,2,1,264,768]{4,3,2,1,0:T(8,128)(2,1)} %copy_bitcast_fusion), channel_id=1, source_target_pairs={{0,4},{4,0},{8,12},{12,8},{1,5},{5,1},{9,13},{13,9},{2,6},{6,2},{1... | collective-permute-start | bytes 4866056 | tf_op jit(solution)/shard_map/ppermute | solution.py:158
  117.9 6.6 %collective-permute-start.17 = (bf16[192,256]{1,0:T(8,128)(2,1)S(1)}, bf16[192,256]{1,0:T(8,128)(2,1)S(1)}, u32[]{:S(2)}, u32[]{:S(2)}) collective-permute-start(bf16[192,256]{1,0:T(8,128)(2,1)S(1)} %get-tuple-element.220), channel_id=1, source_target_pairs={{0,3},{1,2},{2,1},{3,0},{4,7},{5,6},{6,5},{7,4},{8,11},{9,10},{10,... | collective-permute-start | bytes 294920 | tf_op jit(solution)/shard_map/ppermute | solution.py:158
  119.6 11.2 %collective-permute-start.16 = (bf16[192,256]{1,0:T(8,128)(2,1)S(1)}, bf16[192,256]{1,0:T(8,128)(2,1)S(1)}, u32[]{:S(2)}, u32[]{:S(2)}) collective-permute-start(bf16[192,256]{1,0:T(8,128)(2,1)S(1)} %get-tuple-element.221), channel_id=1, source_target_pairs={{0,2},{1,3},{2,0},{3,1},{4,6},{5,7},{6,4},{7,5},{8,10},{9,11},{10,... | collective-permute-start | bytes 294920 | tf_op jit(solution)/shard_map/ppermute | solution.py:158
  123.3 7.5 %collective-permute-start.15 = (bf16[192,256]{1,0:T(8,128)(2,1)S(1)}, bf16[192,256]{1,0:T(8,128)(2,1)S(1)}, u32[]{:S(2)}, u32[]{:S(2)}) collective-permute-start(bf16[192,256]{1,0:T(8,128)(2,1)S(1)} %get-tuple-element.222), channel_id=1, source_target_pairs={{0,1},{1,0},{2,3},{3,2},{4,5},{5,4},{6,7},{7,6},{8,9},{9,8},{10,11... | collective-permute-start | bytes 294920 | tf_op jit(solution)/shard_map/ppermute | solution.py:158
  124.5 29.3 %collective-permute-start.22 = (bf16[4,1,144,768]{3,2,1,0:T(8,128)(2,1)S(1)}, bf16[4,1,144,768]{3,2,1,0:T(8,128)(2,1)S(1)}, u32[]{:S(2)}, u32[]{:S(2)}) collective-permute-start(bf16[4,1,144,768]{3,2,1,0:T(8,128)(2,1)S(1)} %maximum_bitcast_fusion.1), channel_id=1, source_target_pairs={{0,8},{4,12},{8,0},{12,4},{1,9},{5,13},{9,1},{13,5},{2,10},{6,14},... | collective-permute-start | bytes 2654216 | tf_op jit(solution)/shard_map/ppermute | solution.py:158
  153.9 16.2 %collective-permute-start.26 = (bf16[4,2,272,768]{3,2,0,1:T(8,128)(2,1)}, bf16[4,2,272,768]{3,2,0,1:T(8,128)(2,1)}, u32[]{:S(2)}, u32[]{:S(2)}) collective-permute-start(bf16[4,2,272,768]{3,2,0,1:T(8,128)(2,1)} %get-tuple-element.237), channel_id=1, source_target_pairs={{0,4},{4,0},{8,12},{12,8},{1,5},{5,1},{9,13},{13,9},{2,6},{6,2},{1... | collective-permute-start | bytes 10027016 | tf_op jit(solution)/shard_map/ppermute | solution.py:158
  158.3 8.8 %collective-permute-start.40 = (bf16[4,2,1,144,768]{4,3,2,1,0:T(8,128)(2,1)}, bf16[4,2,1,144,768]{4,3,2,1,0:T(8,128)(2,1)}, u32[]{:S(2)}, u32[]{:S(2)}) collective-permute-start(bf16[4,2,1,144,768]{4,3,2,1,0:T(8,128)(2,1)} %bitcast.65), channel_id=1, source_target_pairs={{0,4},{4,0},{8,12},{12,8},{1,5},{5,1},{9,13},{13,9},{2,6},{6,2},{1... | collective-permute-start | bytes 5308424 | tf_op jit(solution)/shard_map/ppermute | solution.py:158
  159.3 14.9 %collective-permute-start.23 = (bf16[192,256]{1,0:T(8,128)(2,1)S(1)}, bf16[192,256]{1,0:T(8,128)(2,1)S(1)}, u32[]{:S(2)}, u32[]{:S(2)}) collective-permute-start(bf16[192,256]{1,0:T(8,128)(2,1)S(1)} %get-tuple-element.217), channel_id=1, source_target_pairs={{0,1},{1,0},{2,3},{3,2},{4,5},{5,4},{6,7},{7,6},{8,9},{9,8},{10,11... | collective-permute-start | bytes 294920 | tf_op jit(solution)/shard_map/ppermute | solution.py:158
  159.4 14.8 %collective-permute-start.24 = (bf16[192,256]{1,0:T(8,128)(2,1)S(1)}, bf16[192,256]{1,0:T(8,128)(2,1)S(1)}, u32[]{:S(2)}, u32[]{:S(2)}) collective-permute-start(bf16[192,256]{1,0:T(8,128)(2,1)S(1)} %get-tuple-element.216), channel_id=1, source_target_pairs={{0,2},{1,3},{2,0},{3,1},{4,6},{5,7},{6,4},{7,5},{8,10},{9,11},{10,... | collective-permute-start | bytes 294920 | tf_op jit(solution)/shard_map/ppermute | solution.py:158
  161.6 12.6 %collective-permute-start.25 = (bf16[192,256]{1,0:T(8,128)(2,1)S(1)}, bf16[192,256]{1,0:T(8,128)(2,1)S(1)}, u32[]{:S(2)}, u32[]{:S(2)}) collective-permute-start(bf16[192,256]{1,0:T(8,128)(2,1)S(1)} %get-tuple-element.215), channel_id=1, source_target_pairs={{0,3},{1,2},{2,1},{3,0},{4,7},{5,6},{6,5},{7,4},{8,11},{9,10},{10,... | collective-permute-start | bytes 294920 | tf_op jit(solution)/shard_map/ppermute | solution.py:158
  174.7 20.2 %collective-permute-start.27 = (bf16[2,272,768]{2,1,0:T(8,128)(2,1)S(1)}, bf16[2,272,768]{2,1,0:T(8,128)(2,1)S(1)}, u32[]{:S(2)}, u32[]{:S(2)}) collective-permute-start(bf16[2,272,768]{2,1,0:T(8,128)(2,1)S(1)} %dynamic-slice_bitcast_fusion), channel_id=1, source_target_pairs={{0,8},{4,12},{8,0},{12,4},{1,9},{5,13},{9,1},{13,5},{2,10},{6,14},... | collective-permute-start | bytes 2506760 | tf_op jit(solution)/shard_map/ppermute | solution.py:158
  176.4 19.9 %collective-permute-start.28 = (bf16[2,2,272,384]{3,2,0,1:T(8,128)(2,1)S(1)}, bf16[2,2,272,384]{3,2,0,1:T(8,128)(2,1)S(1)}, u32[]{:S(2)}, u32[]{:S(2)}) collective-permute-start(bf16[2,2,272,384]{3,2,0,1:T(8,128)(2,1)S(1)} %constant_dynamic-slice_fusion), channel_id=1, source_target_pairs={{0,16},{16,0},{1,17},{17,1},{2,18},{18,2},{3,19},{19,3},{4,20},{20... | collective-permute-start | bytes 2506760 | tf_op jit(solution)/shard_map/ppermute | solution.py:158
  196.6 11.5 %collective-permute-start.29 = (bf16[2,272,384]{2,1,0:T(8,128)(2,1)S(1)}, bf16[2,272,384]{2,1,0:T(8,128)(2,1)S(1)}, u32[]{:S(2)}, u32[]{:S(2)}) collective-permute-start(bf16[2,272,384]{2,1,0:T(8,128)(2,1)S(1)} %dynamic-slice_convert_fusion.1), channel_id=1, source_target_pairs={{0,16},{16,0},{1,17},{17,1},{2,18},{18,2},{3,19},{19,3},{4,20},{20... | collective-permute-start | bytes 1253384 | tf_op jit(solution)/shard_map/ppermute | solution.py:158
  198.2 9.8 %collective-permute-start.30 = (bf16[2,272,384]{2,1,0:T(8,128)(2,1)S(1)}, bf16[2,272,384]{2,1,0:T(8,128)(2,1)S(1)}, u32[]{:S(2)}, u32[]{:S(2)}) collective-permute-start(bf16[2,272,384]{2,1,0:T(8,128)(2,1)S(1)} %fusion.55), channel_id=1, source_target_pairs={{0,8},{4,12},{8,0},{12,4},{1,9},{5,13},{9,1},{13,5},{2,10},{6,14},... | collective-permute-start | bytes 1253384 | tf_op jit(solution)/shard_map/ppermute | solution.py:158
  208.2 15.4 %collective-permute-start.31 = (bf16[3,128,1024]{2,1,0:T(8,128)(2,1)S(1)}, bf16[3,128,1024]{2,1,0:T(8,128)(2,1)S(1)}, u32[]{:S(2)}, u32[]{:S(2)}) collective-permute-start(bf16[3,128,1024]{2,1,0:T(8,128)(2,1)S(1)} %get-tuple-element.125), channel_id=1, source_target_pairs={{0,4},{4,0},{8,12},{12,8},{1,5},{5,1},{9,13},{13,9},{2,6},{6,2},{1... | collective-permute-start | bytes 2359304 | tf_op jit(solution)/shard_map/ppermute | solution.py:158
  208.3 22.9 %collective-permute-start.34 = (bf16[272,384]{1,0:T(8,128)(2,1)S(1)}, bf16[272,384]{1,0:T(8,128)(2,1)S(1)}, u32[]{:S(2)}, u32[]{:S(2)}) collective-permute-start(bf16[272,384]{1,0:T(8,128)(2,1)S(1)} %fusion.63), channel_id=1, source_target_pairs={{0,1},{1,0},{2,3},{3,2},{4,5},{5,4},{6,7},{7,6},{8,9},{9,8},{10,11... | collective-permute-start | bytes 626696 | tf_op jit(solution)/shard_map/ppermute | solution.py:158
  210.1 19.7 %collective-permute-start.33 = (bf16[3,128,1024]{2,1,0:T(8,128)(2,1)S(1)}, bf16[3,128,1024]{2,1,0:T(8,128)(2,1)S(1)}, u32[]{:S(2)}, u32[]{:S(2)}) collective-permute-start(bf16[3,128,1024]{2,1,0:T(8,128)(2,1)S(1)} %add_convert_fusion.1), channel_id=1, source_target_pairs={{0,8},{4,12},{8,0},{12,4},{1,9},{5,13},{9,1},{13,5},{2,10},{6,14},... | collective-permute-start | bytes 2359304 | tf_op jit(solution)/shard_map/ppermute | solution.py:158
  211.7 19.5 %collective-permute-start.35 = (bf16[272,384]{1,0:T(8,128)(2,1)S(1)}, bf16[272,384]{1,0:T(8,128)(2,1)S(1)}, u32[]{:S(2)}, u32[]{:S(2)}) collective-permute-start(bf16[272,384]{1,0:T(8,128)(2,1)S(1)} %get-tuple-element.212), channel_id=1, source_target_pairs={{0,2},{1,3},{2,0},{3,1},{4,6},{5,7},{6,4},{7,5},{8,10},{9,11},{10,... | collective-permute-start | bytes 626696 | tf_op jit(solution)/shard_map/ppermute | solution.py:158
  212.3 18.9 %collective-permute-start.36 = (bf16[272,384]{1,0:T(8,128)(2,1)S(1)}, bf16[272,384]{1,0:T(8,128)(2,1)S(1)}, u32[]{:S(2)}, u32[]{:S(2)}) collective-permute-start(bf16[272,384]{1,0:T(8,128)(2,1)S(1)} %get-tuple-element.211), channel_id=1, source_target_pairs={{0,3},{1,2},{2,1},{3,0},{4,7},{5,6},{6,5},{7,4},{8,11},{9,10},{10,... | collective-permute-start | bytes 626696 | tf_op jit(solution)/shard_map/ppermute | solution.py:158
  233.6 6.4 %collective-permute-start.49 = (bf16[1,1,272,384]{3,2,1,0:T(8,128)(2,1)S(1)}, bf16[1,1,272,384]{3,2,1,0:T(8,128)(2,1)S(1)}, u32[]{:S(2)}, u32[]{:S(2)}) collective-permute-start(bf16[1,1,272,384]{3,2,1,0:T(8,128)(2,1)S(1)} %fusion.62), channel_id=1, source_target_pairs={{0,8},{4,12},{8,0},{12,4},{1,9},{5,13},{9,1},{13,5},{2,10},{6,14},... | collective-permute-start | bytes 626696 | tf_op jit(solution)/shard_map/ppermute | solution.py:158
  235.3 11.9 %collective-permute-start.39 = (bf16[576,256]{1,0:T(8,128)(2,1)S(1)}, bf16[576,256]{1,0:T(8,128)(2,1)S(1)}, u32[]{:S(2)}, u32[]{:S(2)}) collective-permute-start(bf16[576,256]{1,0:T(8,128)(2,1)S(1)} %get-tuple-element.180), channel_id=1, source_target_pairs={{0,3},{1,2},{2,1},{3,0},{4,7},{5,6},{6,5},{7,4},{8,11},{9,10},{10,... | collective-permute-start | bytes 884744 | tf_op jit(solution)/shard_map/ppermute | solution.py:158
  236.7 25.3 %collective-permute-start.38 = (bf16[576,256]{1,0:T(8,128)(2,1)S(1)}, bf16[576,256]{1,0:T(8,128)(2,1)S(1)}, u32[]{:S(2)}, u32[]{:S(2)}) collective-permute-start(bf16[576,256]{1,0:T(8,128)(2,1)S(1)} %get-tuple-element.181), channel_id=1, source_target_pairs={{0,2},{1,3},{2,0},{3,1},{4,6},{5,7},{6,4},{7,5},{8,10},{9,11},{10,... | collective-permute-start | bytes 884744 | tf_op jit(solution)/shard_map/ppermute | solution.py:158
  237.1 24.9 %collective-permute-start.37 = (bf16[576,256]{1,0:T(8,128)(2,1)S(1)}, bf16[576,256]{1,0:T(8,128)(2,1)S(1)}, u32[]{:S(2)}, u32[]{:S(2)}) collective-permute-start(bf16[576,256]{1,0:T(8,128)(2,1)S(1)} %get-tuple-element.182), channel_id=1, source_target_pairs={{0,1},{1,0},{2,3},{3,2},{4,5},{5,4},{6,7},{7,6},{8,9},{9,8},{10,11... | collective-permute-start | bytes 884744 | tf_op jit(solution)/shard_map/ppermute | solution.py:158
  239.8 24.6 %collective-permute-start.41 = (bf16[2,144,768]{2,1,0:T(8,128)(2,1)S(1)}, bf16[2,144,768]{2,1,0:T(8,128)(2,1)S(1)}, u32[]{:S(2)}, u32[]{:S(2)}) collective-permute-start(bf16[2,144,768]{2,1,0:T(8,128)(2,1)S(1)} %dynamic-slice_bitcast_fusion.1), channel_id=1, source_target_pairs={{0,4},{4,0},{8,12},{12,8},{1,5},{5,1},{9,13},{13,9},{2,6},{6,2},{1... | collective-permute-start | bytes 1327112 | tf_op jit(solution)/shard_map/ppermute | solution.py:158
  240.1 26.2 %collective-permute-start.50 = (bf16[1,2,1,272,384]{4,3,2,1,0:T(8,128)(2,1)S(1)}, bf16[1,2,1,272,384]{4,3,2,1,0:T(8,128)(2,1)S(1)}, u32[]{:S(2)}, u32[]{:S(2)}) collective-permute-start(bf16[1,2,1,272,384]{4,3,2,1,0:T(8,128)(2,1)S(1)} %maximum_bitcast_fusion.3), channel_id=1, source_target_pairs={{0,4},{4,0},{8,12},{12,8},{1,5},{5,1},{9,13},{13,9},{2,6},{6,2},{1... | collective-permute-start | bytes 1253384 | tf_op jit(solution)/shard_map/ppermute | solution.py:158
  264.5 6.5 %collective-permute-start.42 = (bf16[144,768]{1,0:T(8,128)(2,1)S(1)}, bf16[144,768]{1,0:T(8,128)(2,1)S(1)}, u32[]{:S(2)}, u32[]{:S(2)}) collective-permute-start(bf16[144,768]{1,0:T(8,128)(2,1)S(1)} %dynamic-slice_bitcast_fusion.2), channel_id=1, source_target_pairs={{0,8},{4,12},{8,0},{12,4},{1,9},{5,13},{9,1},{13,5},{2,10},{6,14},... | collective-permute-start | bytes 663560 | tf_op jit(solution)/shard_map/ppermute | solution.py:158
  271.1 4.8 %collective-permute-start.43 = (bf16[144,384]{1,0:T(8,128)(2,1)S(1)}, bf16[144,384]{1,0:T(8,128)(2,1)S(1)}, u32[]{:S(2)}, u32[]{:S(2)}) collective-permute-start(bf16[144,384]{1,0:T(8,128)(2,1)S(1)} %dynamic-slice_convert_fusion.2), channel_id=1, source_target_pairs={{0,16},{16,0},{1,17},{17,1},{2,18},{18,2},{3,19},{19,3},{4,20},{20... | collective-permute-start | bytes 331784 | tf_op jit(solution)/shard_map/ppermute | solution.py:158
  276.9 5.4 %collective-permute-start.46 = (f32[1,384]{1,0:T(1,128)S(1)}, f32[1,384]{1,0:T(1,128)S(1)}, u32[]{:S(2)}, u32[]{:S(2)}) collective-permute-start(f32[1,384]{1,0:T(1,128)S(1)} %broadcast_in_dim.48), channel_id=1, source_target_pairs={{0,3},{1,2},{2,1},{3,0},{4,7},{5,6},{6,5},{7,4},{8,11},{9,10},{10,... | collective-permute-start | bytes 4616 | tf_op jit(solution)/shard_map/ppermute | solution.py:158
  278.0 4.9 %collective-permute-start.44 = (f32[1,384]{1,0:T(1,128)S(1)}, f32[1,384]{1,0:T(1,128)S(1)}, u32[]{:S(2)}, u32[]{:S(2)}) collective-permute-start(f32[1,384]{1,0:T(1,128)S(1)} %broadcast_in_dim.48), channel_id=1, source_target_pairs={{0,1},{1,0},{2,3},{3,2},{4,5},{5,4},{6,7},{7,6},{8,9},{9,8},{10,11... | collective-permute-start | bytes 4616 | tf_op jit(solution)/shard_map/ppermute | solution.py:158
  283.0 4.9 %collective-permute-start.47 = (bf16[1,1,160,384]{3,2,1,0:T(8,128)(2,1)S(1)}, bf16[1,1,160,384]{3,2,1,0:T(8,128)(2,1)S(1)}, u32[]{:S(2)}, u32[]{:S(2)}) collective-permute-start(bf16[1,1,160,384]{3,2,1,0:T(8,128)(2,1)S(1)} %pad_maximum_fusion.20), channel_id=1, source_target_pairs={{0,8},{4,12},{8,0},{12,4},{1,9},{5,13},{9,1},{13,5},{2,10},{6,14},... | collective-permute-start | bytes 368648 | tf_op jit(solution)/shard_map/ppermute | solution.py:158
  (54 other events, 337.0 us)
